TPU v7x, 32 devices: a whole 2x2x4 slice. The times are simulated.
32 devices in a mesh: groups: 2 (over y), expert: 4 (over z), dp: 2 (over x), sub: 2 (over core).
Axes of the slice: x: 2, y: 2, z: 4, core: 2. Of those that a mesh axis runs over, the one named last changes fastest.
Arguments:
- tokens: bfloat16 [4096, 1536], P(('groups', 'expert', 'dp', 'sub')), parts along dimension 0, may hold values from -6 to 6
- expert_ids: int32 [4096, 2], P(('groups', 'expert', 'dp', 'sub')), parts along dimension 0, may hold values from 0 to 7, all different within a row; in each aligned block of 128 rows (0 to 127, 128 to 255, ...) at most 48 rows name the same one
- route_weights: bfloat16 [4096, 2], P(('groups', 'expert', 'dp', 'sub')), parts along dimension 0, may hold values from 0.125 to 1
- out_grad: bfloat16 [4096, 1536], P(('groups', 'expert', 'dp', 'sub')), parts along dimension 0, may hold values from -6 to 6
- gate_weight: bfloat16 [8, 384, 1536], P(('expert', 'dp'), 'sub'), may hold values from -0.15625 to 0.15625
- up_weight: bfloat16 [8, 384, 1536], P(('expert', 'dp'), 'sub'), may hold values from -0.15625 to 0.15625
- down_weight: bfloat16 [8, 384, 1536], P(('expert', 'dp'), 'sub'), may hold values from -0.3125 to 0.3125
Outputs:
- mixed: bfloat16 [4096, 1536], P(('groups', 'expert', 'dp', 'sub')), parts along dimension 0
- token_grad: bfloat16 [4096, 1536], P(('groups', 'expert', 'dp', 'sub')), parts along dimension 0
- route_grad: float32 [4096, 2], P(('groups', 'expert', 'dp', 'sub')), parts along dimension 0
- gate_grad: bfloat16 [16, 384, 1536], P(('groups', 'expert', 'dp'), 'sub'), parts along dimension 0
- up_grad: bfloat16 [16, 384, 1536], P(('groups', 'expert', 'dp'), 'sub'), parts along dimension 0
- down_grad: bfloat16 [16, 384, 1536], P(('groups', 'expert', 'dp'), 'sub'), parts along dimension 0
There are 2 independent parts, one for each index of `groups`. A program takes and returns all parts, laid end to end along the dimension named above; an argument that names none is the same for every part. Nothing has to cross between parts.
Inputs may be any that keep to these rules, and one draw needn't show every extreme that they name: `expert_ids`: each row names 2 different experts. In the rows of one device (aligned blocks of 128 rows) no expert is named by more than 48 rows, a bound that some block reaches.
All inputs are finite; a program needn't handle non-finite values.
Results may differ from a plain program's by a relative error of at most 0.009.
Values may be sent and summed in bfloat16 or wider, within the bound.
A program may use at most 64 MiB of HBM per device.

v0:
```python
import jax
import jax.numpy as jnp
from jax import lax
from jax.sharding import PartitionSpec as P


def expert_piece(rows_x, rows_grad, gate_piece, up_piece, down_piece):
    gate = jnp.einsum("rd,fd->rf", rows_x, gate_piece, preferred_element_type=jnp.float32)
    up_value = jnp.einsum("rd,fd->rf", rows_x, up_piece, preferred_element_type=jnp.float32)
    sigmoid = jax.nn.sigmoid(gate)
    hidden = (gate * sigmoid * up_value).astype(jnp.bfloat16)
    output = jnp.einsum("rf,fd->rd", hidden, down_piece, preferred_element_type=jnp.float32)
    hidden_grad = jnp.einsum("rd,fd->rf", rows_grad, down_piece, preferred_element_type=jnp.float32)
    gate_delta = (hidden_grad * up_value * sigmoid * (1.0 + gate * (1.0 - sigmoid))).astype(
        jnp.bfloat16
    )
    up_delta = (hidden_grad * gate * sigmoid).astype(jnp.bfloat16)
    input_grad = jnp.einsum(
        "rf,fd->rd", gate_delta, gate_piece, preferred_element_type=jnp.float32
    ) + jnp.einsum("rf,fd->rd", up_delta, up_piece, preferred_element_type=jnp.float32)
    gate_part = jnp.einsum("rf,rd->fd", gate_delta, rows_x, preferred_element_type=jnp.float32)
    up_part = jnp.einsum("rf,rd->fd", up_delta, rows_x, preferred_element_type=jnp.float32)
    down_part = jnp.einsum("rf,rd->fd", hidden, rows_grad, preferred_element_type=jnp.float32)
    return (output, input_grad, gate_part, up_part, down_part)


def shards(tokens, expert_ids, route_weights, out_grad, gate_weight, up_weight, down_weight):
    tok_rows, features = tokens.shape
    top_count = expert_ids.shape[1]
    expert_count = lax.axis_size("expert")
    replica_count = lax.axis_size("dp")
    experts = expert_count * replica_count
    capacity = max(2, 3 * tok_rows * top_count // (2 * experts))
    flat_ids = expert_ids.reshape(-1)
    onehot = (flat_ids[:, None] == jnp.arange(experts, dtype=jnp.int32)[None, :]).astype(jnp.int32)
    before = jnp.cumsum(onehot, axis=0) - onehot
    slot_index = jnp.sum(before * onehot, axis=1)
    target = flat_ids * capacity + slot_index
    rows_total = experts * capacity
    send_x = (
        jnp.zeros((rows_total, features), jnp.bfloat16)
        .at[target]
        .set(jnp.repeat(tokens, top_count, axis=0))
    )
    send_dy = (
        jnp.zeros((rows_total, features), jnp.bfloat16)
        .at[target]
        .set(jnp.repeat(out_grad, top_count, axis=0))
    )
    send_w = jnp.zeros((rows_total,), jnp.bfloat16).at[target].set(route_weights.reshape(-1))
    moved = (
        lax.all_to_all(
            send_x.reshape(experts, capacity, features),
            ("expert", "dp"),
            split_axis=0,
            concat_axis=0,
            tiled=True,
        ),
        lax.all_to_all(
            send_dy.reshape(experts, capacity, features),
            ("expert", "dp"),
            split_axis=0,
            concat_axis=0,
            tiled=True,
        ),
        lax.all_to_all(
            send_w.reshape(experts, capacity),
            ("expert", "dp"),
            split_axis=0,
            concat_axis=0,
            tiled=True,
        ),
    )
    recv_x = moved[0].reshape(rows_total, features)
    recv_dy = moved[1].reshape(rows_total, features)
    recv_w = moved[2].reshape(rows_total)
    scaled_grad = (recv_w[:, None].astype(jnp.float32) * recv_dy.astype(jnp.float32)).astype(
        jnp.bfloat16
    )
    out_part, grad_part, gate_part, up_part, down_part = expert_piece(
        recv_x,
        scaled_grad,
        lax.all_gather(gate_weight, "sub", axis=1, tiled=True)[0],
        lax.all_gather(up_weight, "sub", axis=1, tiled=True)[0],
        lax.all_gather(down_weight, "sub", axis=1, tiled=True)[0],
    )
    outputs = out_part.astype(jnp.bfloat16)
    input_grads = grad_part.astype(jnp.bfloat16)
    summed = (
        lax.psum_scatter(
            gate_part.astype(jnp.bfloat16), "sub", scatter_dimension=0, tiled=True
        ).astype(jnp.float32),
        lax.psum_scatter(
            up_part.astype(jnp.bfloat16), "sub", scatter_dimension=0, tiled=True
        ).astype(jnp.float32),
        lax.psum_scatter(
            down_part.astype(jnp.bfloat16), "sub", scatter_dimension=0, tiled=True
        ).astype(jnp.float32),
    )
    gate_grad = summed[0].astype(jnp.bfloat16)[None]
    up_grad = summed[1].astype(jnp.bfloat16)[None]
    down_grad = summed[2].astype(jnp.bfloat16)[None]
    returned = (
        lax.all_to_all(
            outputs.reshape(experts, capacity, features),
            ("expert", "dp"),
            split_axis=0,
            concat_axis=0,
            tiled=True,
        ),
        lax.all_to_all(
            input_grads.reshape(experts, capacity, features),
            ("expert", "dp"),
            split_axis=0,
            concat_axis=0,
            tiled=True,
        ),
    )
    back_out = returned[0].reshape(rows_total, features)[target]
    back_grad = returned[1].reshape(rows_total, features)[target]
    weights_flat = route_weights.reshape(-1).astype(jnp.float32)
    mixed = jnp.sum(
        (weights_flat[:, None] * back_out.astype(jnp.float32)).reshape(
            tok_rows, top_count, features
        ),
        axis=1,
    ).astype(jnp.bfloat16)
    token_grad = jnp.sum(
        back_grad.astype(jnp.float32).reshape(tok_rows, top_count, features), axis=1
    ).astype(jnp.bfloat16)
    route_grad = jnp.sum(
        jnp.repeat(out_grad, top_count, axis=0).astype(jnp.float32) * back_out.astype(jnp.float32),
        axis=1,
    ).reshape(tok_rows, top_count)
    return (mixed, token_grad, route_grad, gate_grad, up_grad, down_grad)


def solution(mesh):
    placed = (
        P(("groups", "expert", "dp", "sub"), None),
        P(("groups", "expert", "dp", "sub"), None),
        P(("groups", "expert", "dp", "sub"), None),
        P(("groups", "expert", "dp", "sub"), None),
        P(("expert", "dp"), "sub", None),
        P(("expert", "dp"), "sub", None),
        P(("expert", "dp"), "sub", None),
    )
    return jax.shard_map(
        shards,
        mesh=mesh,
        in_specs=placed,
        out_specs=(
            P(("groups", "expert", "dp", "sub"), None),
            P(("groups", "expert", "dp", "sub"), None),
            P(("groups", "expert", "dp", "sub"), None),
            P(("groups", "expert", "dp"), "sub", None),
            P(("groups", "expert", "dp"), "sub", None),
            P(("groups", "expert", "dp"), "sub", None),
        ),
        check_vma=False,
    )
```

profile of v0, /device:TPU:0, one launch (start us, length us, event | category | flops | bytes accessed | tf_op | source)
XLA Modules:
  0.0 186.3 jit_solution(11618582123286696355)
XLA Ops:
  11.0 2.2 %scatter_custom_fusion.1 = bf16[384]{0:T(512)(128)(2,1)S(1)} fusion(s32[256]{0:T(256)S(1)} %bitcast.64, bf16[256]{0:T(256)(128)(2,1)S(1)} %reshape.185, bf16[]{:T(256)} %constant.6.clone.1), kind=kCustom, calls=%fused_computation.43 | custom fusion | bytes 770 | tf_op jit(solution)/shard_map/scatter | solution.py:50
  13.9 7.3 %all-to-all-start.2 = ((bf16[8,1,48]{2,1,0:T(2,128)(2,1)}), bf16[8,1,48]{2,1,0:T(2,128)(2,1)S(1)}, u32[]{:S(2)}, u32[]{:S(2)}) async-start(bf16[8,1,48]{2,1,0:T(2,128)(2,1)} %all_to_all.24), calls=%async_computation.2 | async-start | bytes 8192 | tf_op jit(solution)/shard_map/all_to_all | solution.py:66
  21.2 1.4 broadcast_in_dim.30
  22.9 3.0 %scatter_custom_fusion = bf16[384,1536]{1,0:T(8,128)(2,1)} fusion(s32[256]{0:T(256)S(1)} %bitcast.65, bf16[256,1536]{1,0:T(8,128)(2,1)S(1)} %reshape.177, bf16[]{:T(256)} %constant.6.clone.1), kind=kCustom, calls=%fused_computation.32 | custom fusion | bytes 1179650 | tf_op jit(solution)/shard_map/scatter | solution.py:43
  25.8 1.7 all-to-all-done.2
  27.5 4.4 %all-to-all-start = ((bf16[8,48,1536]{2,1,0:T(8,128)(2,1)}), bf16[8,48,1536]{2,1,0:T(8,128)(2,1)S(1)}, u32[]{:S(2)}, u32[]{:S(2)}) async-start(bf16[8,48,1536]{2,1,0:T(8,128)(2,1)} %bitcast.4), calls=%async_computation | async-start | bytes 2359296 | tf_op jit(solution)/shard_map/all_to_all | solution.py:52
  33.4 2.9 %scatter_custom_fusion.2 = bf16[384,1536]{1,0:T(8,128)(2,1)} fusion(s32[256]{0:T(256)S(1)} %bitcast.66, bf16[256,1536]{1,0:T(8,128)(2,1)S(1)} %reshape.193, bf16[]{:T(256)} %constant.6.clone.1), kind=kCustom, calls=%fused_computation.30 | custom fusion | bytes 1179650 | tf_op jit(solution)/shard_map/scatter | solution.py:48
  36.3 23.8 %all-to-all-done = bf16[8,48,1536]{2,1,0:T(8,128)(2,1)S(1)} async-done(((bf16[8,48,1536]{2,1,0:T(8,128)(2,1)}), bf16[8,48,1536]{2,1,0:T(8,128)(2,1)S(1)}, u32[]{:S(2)}, u32[]{:S(2)}) %all-to-all-start) | async-done | bytes 1179680 | tf_op jit(solution)/shard_map/all_to_all | solution.py:52
  60.2 3.6 %all-to-all-start.3 = ((bf16[8,48,1536]{2,1,0:T(8,128)(2,1)}), bf16[8,48,1536]{2,1,0:T(8,128)(2,1)S(1)}, u32[]{:S(2)}, u32[]{:S(2)}) async-start(bf16[8,48,1536]{2,1,0:T(8,128)(2,1)} %bitcast.12), calls=%async_computation.3 | async-start | bytes 2359296 | tf_op jit(solution)/shard_map/all_to_all | solution.py:59
  65.4 2.9 %fusion.10 = f32[384,384]{1,0:T(8,128)} fusion(bf16[384,1536]{1,0:T(8,128)(2,1)S(1)} %bitcast.57, bf16[1,384,1536]{2,1,0:T(8,128)(2,1)} %all-gather.4.cloned.1.call-done), kind=kOutput, calls=%fused_computation.24 | convolution fusion | flops 452984832 | bytes 2949120 | tf_op jit(solution)/shard_map/rd,fd->rf/dot_general | solution.py:8
  68.3 8.5 %all-gather.6.cloned.1.call-done = bf16[1,384,1536]{2,1,0:T(8,128)(2,1)} async-done(((bf16[1,192,1536]{2,1,0:T(8,128)(2,1)}), bf16[1,384,1536]{2,1,0:T(8,128)(2,1)}) %all-gather.6.cloned.1.call-update) | async-done | bytes 1179664 | tf_op jit(solution)/shard_map/all_gather | solution.py:84
  76.8 2.9 %fusion.6 = f32[384,384]{1,0:T(8,128)} fusion(bf16[384,1536]{1,0:T(8,128)(2,1)S(1)} %bitcast.58, bf16[1,384,1536]{2,1,0:T(8,128)(2,1)} %all-gather.6.cloned.1.call-done), kind=kOutput, calls=%fused_computation.20 | convolution fusion | flops 452984832 | bytes 2949120 | tf_op jit(solution)/shard_map/rd,fd->rf/dot_general | solution.py:9
  79.6 12.7 %all-to-all-done.3 = bf16[8,48,1536]{2,1,0:T(8,128)(2,1)S(1)} async-done(((bf16[8,48,1536]{2,1,0:T(8,128)(2,1)}), bf16[8,48,1536]{2,1,0:T(8,128)(2,1)S(1)}, u32[]{:S(2)}, u32[]{:S(2)}) %all-to-all-start.3) | async-done | bytes 1179680 | tf_op jit(solution)/shard_map/all_to_all | solution.py:59
  92.6 1.3 multiply_convert_fusion
  93.9 2.9 %multiply_convert_fusion.1 = (bf16[384,384]{1,0:T(8,128)(2,1)S(1)}, bf16[384,384]{1,0:T(8,128)(2,1)S(1)}, bf16[384,384]{1,0:T(8,128)(2,1)S(1)}) fusion(f32[384,384]{1,0:T(8,128)} %fusion.10, f32[384,384]{1,0:T(8,128)} %fusion.6, bf16[384,1536]{1,0:T(8,128)(2,1)} %bitcast.62, bf16[1,384,1536]{2,1,0:T(8,128)(2,1)} %all-gather.8.cloned.1.call-done), kind=kOutput, calls=%fused_computation.26 | convolution fusion | flops 455344128 | bytes 4423680 | tf_op jit(solution)/shard_map/rd,fd->rf/dot_general | solution.py:13
  96.8 1.8 convolution_convert_fusion
  98.9 1.8 convolution_convert_fusion.2
  102.0 1.8 fusion.8
  103.8 1.8 fusion
  105.6 3.8 %all-to-all-start.4 = ((bf16[8,48,1536]{2,1,0:T(8,128)(2,1)}), bf16[8,48,1536]{2,1,0:T(8,128)(2,1)S(1)}, u32[]{:S(2)}, u32[]{:S(2)}) async-start(bf16[8,48,1536]{2,1,0:T(8,128)(2,1)} %bitcast.14), calls=%async_computation.4 | async-start | bytes 2359296 | tf_op jit(solution)/shard_map/all_to_all | solution.py:111
  109.4 2.7 %convolution_convert_fusion.3 = bf16[384,1536]{1,0:T(8,128)(2,1)} fusion(bf16[384,384]{1,0:T(8,128)(2,1)} %copy-done.7, bf16[1,384,1536]{2,1,0:T(8,128)(2,1)S(1)} %copy-done.6), kind=kOutput, calls=%fused_computation.10 | convolution fusion | flops 453574656 | bytes 2654208 | tf_op jit(solution)/shard_map/rf,fd->rd/dot_general | solution.py:12
  112.2 26.0 %all-to-all-done.4 = bf16[8,48,1536]{2,1,0:T(8,128)(2,1)S(1)} async-done(((bf16[8,48,1536]{2,1,0:T(8,128)(2,1)}), bf16[8,48,1536]{2,1,0:T(8,128)(2,1)S(1)}, u32[]{:S(2)}, u32[]{:S(2)}) %all-to-all-start.4) | async-done | bytes 1179680 | tf_op jit(solution)/shard_map/all_to_all | solution.py:111
  138.2 3.6 %all-to-all-start.1 = ((bf16[8,48,1536]{2,1,0:T(8,128)(2,1)}), bf16[8,48,1536]{2,1,0:T(8,128)(2,1)S(1)}, u32[]{:S(2)}, u32[]{:S(2)}) async-start(bf16[8,48,1536]{2,1,0:T(8,128)(2,1)} %bitcast.61), calls=%async_computation.1 | async-start | bytes 2359296 | tf_op jit(solution)/shard_map/all_to_all | solution.py:104
  141.9 2.8 %convolution_convert_fusion.1 = bf16[384,1536]{1,0:T(8,128)(2,1)} fusion(bf16[384,384]{1,0:T(8,128)(2,1)} %copy-done.4, bf16[384,1536]{1,0:T(8,128)(2,1)S(1)} %bitcast.60), kind=kOutput, calls=%fused_computation.8 | convolution fusion | flops 453574656 | bytes 2654208 | tf_op jit(solution)/shard_map/rf,rd->fd/dot_general | solution.py:22
  145.7 1.6 broadcast_in_dim.33
  147.2 3.2 %broadcast_in_dim.34 = f32[256,1536]{1,0:T(8,128)} reshape(f32[128,2,1536]{2,1,0:T(2,128)} %broadcast_in_dim.33) | data formatting | bytes 3145728 | tf_op jit(solution)/shard_map/broadcast_in_dim | solution.py:48
  150.4 2.2 %gather_fusion.1 = bf16[256,1536]{1,0:T(8,128)(2,1)} fusion(bf16[384,1536]{1,0:T(8,128)(2,1)S(1)} %bitcast.55, s32[1024]{0:T(1024)S(1)} %pad_clamp_fusion), kind=kCustom, calls=%fused_computation.1 | custom fusion | bytes 1573888 | tf_op jit(solution)/shard_map/gather | solution.py:120
  152.6 2.2 %gather.10 = bf16[128,2,1536]{2,1,0:T(2,128)(2,1)S(1)} reshape(bf16[256,1536]{1,0:T(8,128)(2,1)} %gather_fusion.1) | data formatting | bytes 1572864 | tf_op jit(solution)/shard_map/gather | solution.py:120
  154.7 2.9 %reduce_sum.46 = bf16[128,1536]{1,0:T(8,128)(2,1)} reduce(bf16[128,2,1536]{2,1,0:T(2,128)(2,1)S(1)} %gather.10, bf16[]{:T(256)} %constant.6.clone.1), dimensions={1}, to_apply=%region_7.8 | reduce | flops 196608 | bytes 1179650 | tf_op jit(solution)/shard_map/reduce_sum | solution.py:128
  157.6 13.0 %all-to-all-done.1 = bf16[8,48,1536]{2,1,0:T(8,128)(2,1)S(1)} async-done(((bf16[8,48,1536]{2,1,0:T(8,128)(2,1)}), bf16[8,48,1536]{2,1,0:T(8,128)(2,1)S(1)}, u32[]{:S(2)}, u32[]{:S(2)}) %all-to-all-start.1) | async-done | bytes 1179680 | tf_op jit(solution)/shard_map/all_to_all | solution.py:104
  171.8 2.1 %reshape.153 = f32[128,2,1536]{2,1,0:T(2,128)} reshape(bf16[256,1536]{1,0:T(8,128)(2,1)S(1)} %gather_fusion) | data formatting | bytes 2359296 | tf_op jit(solution)/shard_map/convert_element_type | solution.py:123
  175.0 4.4 %multiply_reduce_fusion.1 = bf16[128,1536]{1,0:T(8,128)(2,1)} fusion(f32[128,2,1536]{2,1,0:T(2,128)} %reshape.153, f32[128,2]{1,0:T(8,128)S(1)} %copy.26), kind=kLoop, calls=%fused_computation.15 | loop fusion | flops 589824 | bytes 1967104 | tf_op jit(solution)/shard_map/reduce_sum | solution.py:122
  (66 shorter events, 13.0 us)
Async XLA Ops:
  13.9 13.6 %all-to-all-start.2 = ((bf16[8,1,48]{2,1,0:T(2,128)(2,1)}), bf16[8,1,48]{2,1,0:T(2,128)(2,1)S(1)}, u32[]{:S(2)}, u32[]{:S(2)}) async-start(bf16[8,1,48]{2,1,0:T(2,128)(2,1)} %all_to_all.24), calls=%async_computation.2 | async-start | bytes 8192 | tf_op jit(solution)/shard_map/all_to_all | solution.py:66
  27.5 5.1 %copy-start.1 = (bf16[128,1536]{1,0:T(8,128)(2,1)S(1)}, bf16[128,1536]{1,0:T(8,128)(2,1)}, u32[]{:S(2)}) copy-start(bf16[128,1536]{1,0:T(8,128)(2,1)} %param.10) | copy-start | bytes 1179652
  27.5 32.6 %all-to-all-start = ((bf16[8,48,1536]{2,1,0:T(8,128)(2,1)}), bf16[8,48,1536]{2,1,0:T(8,128)(2,1)S(1)}, u32[]{:S(2)}, u32[]{:S(2)}) async-start(bf16[8,48,1536]{2,1,0:T(8,128)(2,1)} %bitcast.4), calls=%async_computation | async-start | bytes 2359296 | tf_op jit(solution)/shard_map/all_to_all | solution.py:52
  31.9 33.5 %all-gather.4.cloned.1.call-start = ((), (), s32[]{:S(2)}) async-start(), calls=%async_computation.8 | async-start | bytes 1769472 | tf_op jit(solution)/shard_map/all_gather | solution.py:83
  60.2 32.1 %all-to-all-start.3 = ((bf16[8,48,1536]{2,1,0:T(8,128)(2,1)}), bf16[8,48,1536]{2,1,0:T(8,128)(2,1)S(1)}, u32[]{:S(2)}, u32[]{:S(2)}) async-start(bf16[8,48,1536]{2,1,0:T(8,128)(2,1)} %bitcast.12), calls=%async_computation.3 | async-start | bytes 2359296 | tf_op jit(solution)/shard_map/all_to_all | solution.py:59
  63.7 13.0 %all-gather.6.cloned.1.call-start = ((), (), s32[]{:S(2)}) async-start(), calls=%async_computation.9 | async-start | bytes 1769472 | tf_op jit(solution)/shard_map/all_gather | solution.py:84
  64.5 29.4 %all-gather.8.cloned.1.call-start = ((), (), s32[]{:S(2)}) async-start(), calls=%async_computation.10 | async-start | bytes 1769472 | tf_op jit(solution)/shard_map/all_gather | solution.py:85
  65.2 114.2 %reduce-scatter.8.cloned.1.call-start = ((), (), s32[]{:S(2)}) async-start(), calls=%async_computation.13 | async-start | bytes 1769472 | tf_op jit(solution)/shard_map/reduce_scatter | solution.py:96
  96.8 1.9 %copy-start.7 = (bf16[384,384]{1,0:T(8,128)(2,1)}, bf16[384,384]{1,0:T(8,128)(2,1)S(1)}, u32[]{:S(2)}) copy-start(bf16[384,384]{1,0:T(8,128)(2,1)S(1)} %get-tuple-element.26) | copy-start | bytes 884740
  96.8 2.1 %copy-start.8 = (bf16[384,384]{1,0:T(8,128)(2,1)}, bf16[384,384]{1,0:T(8,128)(2,1)S(1)}, u32[]{:S(2)}) copy-start(bf16[384,384]{1,0:T(8,128)(2,1)S(1)} %get-tuple-element.25) | copy-start | bytes 884740
  96.8 7.0 %copy-start.4 = (bf16[384,384]{1,0:T(8,128)(2,1)}, bf16[384,384]{1,0:T(8,128)(2,1)S(1)}, u32[]{:S(2)}) copy-start(bf16[384,384]{1,0:T(8,128)(2,1)S(1)} %get-tuple-element.24) | copy-start | bytes 884740
  98.7 80.8 %reduce-scatter.4.cloned.1.call-start = ((), (), s32[]{:S(2)}) async-start(), calls=%async_computation.11 | async-start | bytes 1769472 | tf_op jit(solution)/shard_map/reduce_scatter | solution.py:90
  100.7 1.3 copy-start.5
  102.0 1.8 copy-start.3
  105.6 3.8 %copy-start.6 = (bf16[1,384,1536]{2,1,0:T(8,128)(2,1)S(1)}, bf16[1,384,1536]{2,1,0:T(8,128)(2,1)}, u32[]{:S(2)}) copy-start(bf16[1,384,1536]{2,1,0:T(8,128)(2,1)} %all-gather.8.cloned.1.call-done) | copy-start | bytes 3538948
  105.6 32.5 %all-to-all-start.4 = ((bf16[8,48,1536]{2,1,0:T(8,128)(2,1)}), bf16[8,48,1536]{2,1,0:T(8,128)(2,1)S(1)}, u32[]{:S(2)}, u32[]{:S(2)}) async-start(bf16[8,48,1536]{2,1,0:T(8,128)(2,1)} %bitcast.14), calls=%async_computation.4 | async-start | bytes 2359296 | tf_op jit(solution)/shard_map/all_to_all | solution.py:111
  138.2 32.4 %all-to-all-start.1 = ((bf16[8,48,1536]{2,1,0:T(8,128)(2,1)}), bf16[8,48,1536]{2,1,0:T(8,128)(2,1)S(1)}, u32[]{:S(2)}, u32[]{:S(2)}) async-start(bf16[8,48,1536]{2,1,0:T(8,128)(2,1)} %bitcast.61), calls=%async_computation.1 | async-start | bytes 2359296 | tf_op jit(solution)/shard_map/all_to_all | solution.py:104
  141.8 37.6 %reduce-scatter.6.cloned.1.call-start = ((), (), s32[]{:S(2)}) async-start(), calls=%async_computation.12 | async-start | bytes 1769472 | tf_op jit(solution)/shard_map/reduce_scatter | solution.py:93
  144.7 0.7 copy-start.9
  144.7 1.0 copy-start.2
  171.8 2.1 %copy-start = (f32[256,1536]{1,0:T(8,128)S(1)}, f32[256,1536]{1,0:T(8,128)}, u32[]{:S(2)}) copy-start(f32[256,1536]{1,0:T(8,128)} %broadcast_in_dim.34) | copy-start | bytes 4718596
Sparse Core Ops, SparseCore 0:
  34.3 10.6 all-gather.3
  66.1 10.5 all-gather.5
  78.3 10.3 all-gather.7
  98.8 7.7 reduce-scatter.7
  109.3 9.8 reduce-scatter.3
  145.1 10.0 reduce-scatter.5
where the time goes:
time: 187 us; the launch traced here: 186 us
  waiting for transfers between devices  87.8 us (47%)
  local copies, waits for them, and re-layouts  29.2 us (16%)
  starting transfers between devices  23 us (12%)
  matrix products  21.5 us (11%)
  between operations  14.3 us (8%)
  other arithmetic  10.5 us (6%)
    all_to_all x1, waiting for transfers between devices, shards(): lax.all_to_all(input_grads.reshape(experts, capacity, features), ('expert...  26 us
    all_to_all x1, waiting for transfers between devices, shards(): lax.all_to_all(send_x.reshape(experts, capacity, features), ('expert', 'd...  23.8 us
    all_to_all x1, waiting for transfers between devices, shards(): lax.all_to_all(outputs.reshape(experts, capacity, features), ('expert', '...  13 us
    all_to_all x1, waiting for transfers between devices, shards(): lax.all_to_all(send_dy.reshape(experts, capacity, features), ('expert', '...  12.7 us
    all_gather x1, waiting for transfers between devices, shards(): lax.all_gather(up_weight, 'sub', axis=1, tiled=True)[0]  8.46 us
    all_to_all x1, starting transfers between devices, shards(): lax.all_to_all(send_w.reshape(experts, capacity), ('expert', 'dp'), split...  7.25 us
    broadcast_in_dim x3, local copies, waits for them, and re-layouts, shards(): jnp.repeat(out_grad, top_count, axis=0)  5.13 us
    reduce_sum x1, other arithmetic, shards(): jnp.sum((weights_flat[:, None] * back_out.astype(jnp.float32)).reshape(to...  4.42 us
  transfers between devices with their start and end apart: 11, of which 6 were waited for; matrix products, arithmetic and copies ran while one was open for 26% of the time, Pallas kernels for 0%

commit v1 on v0

--- a/solution.py
+++ b/solution.py
@@ -135,6 +135,56 @@
     return (mixed, token_grad, route_grad, gate_grad, up_grad, down_grad)
 
 
+def shards_dense(tokens, expert_ids, route_weights, out_grad, gate_weight, up_weight, down_weight):
+    rows, features = tokens.shape
+    dp = lax.axis_size("dp")
+    stages = lax.axis_size("expert")
+    experts = stages * dp
+    half = gate_weight.shape[1]
+    f32, bf16 = jnp.float32, jnp.bfloat16
+    which = jnp.arange(experts, dtype=jnp.int32)
+    hit = expert_ids[:, :, None] == which[None, None, :]
+    by_expert = jnp.sum(jnp.where(hit, route_weights.astype(f32)[:, :, None], 0.0), axis=1).astype(bf16)
+    w_all = lax.all_gather(by_expert, "expert", axis=0, tiled=True)
+    x_all = lax.all_gather(tokens, "expert", axis=0, tiled=True)
+    gate_w = lax.all_gather(gate_weight[0], ("dp", "sub"), axis=0, tiled=True)
+    up_w = lax.all_gather(up_weight[0], ("dp", "sub"), axis=0, tiled=True)
+    down_w = lax.all_gather(down_weight[0], ("dp", "sub"), axis=0, tiled=True)
+    dy_all = lax.all_gather(out_grad, "expert", axis=0, tiled=True)
+    units = gate_w.shape[0]
+    mine = lax.dynamic_slice_in_dim(w_all, lax.axis_index("expert") * dp, dp, axis=1).astype(f32)
+    w_units = jnp.repeat(mine, units // dp, axis=1)
+    gate = jnp.einsum("rd,fd->rf", x_all, gate_w, preferred_element_type=f32)
+    up = jnp.einsum("rd,fd->rf", x_all, up_w, preferred_element_type=f32)
+    sig = jax.nn.sigmoid(gate)
+    hidden = gate * sig * up
+    scaled = (w_units * hidden).astype(bf16)
+    mixed_part = jnp.einsum("rf,fd->rd", scaled, down_w, preferred_element_type=f32).astype(bf16)
+    mixed = lax.psum_scatter(mixed_part, "expert", scatter_dimension=0, tiled=True)
+    back = jnp.einsum("rd,fd->rf", dy_all, down_w, preferred_element_type=f32)
+    route = jnp.sum((hidden * back).reshape(stages, rows, dp, units // dp), axis=3)
+    hidden_grad = w_units * back
+    gate_delta = (hidden_grad * up * sig * (1.0 + gate * (1.0 - sig))).astype(bf16)
+    up_delta = (hidden_grad * gate * sig).astype(bf16)
+    token_part = (
+        jnp.einsum("rf,fd->rd", gate_delta, gate_w, preferred_element_type=f32)
+        + jnp.einsum("rf,fd->rd", up_delta, up_w, preferred_element_type=f32)
+    ).astype(bf16)
+    token_grad = lax.psum_scatter(token_part, "expert", scatter_dimension=0, tiled=True)
+
+    def weight_grad(left, right):
+        part = jnp.einsum("rf,rd->fd", left, right, preferred_element_type=f32).astype(bf16)
+        return lax.psum_scatter(part, ("dp", "sub"), scatter_dimension=0, tiled=True)[None]
+
+    down_grad = weight_grad(scaled, dy_all)
+    gate_grad = weight_grad(gate_delta, x_all)
+    up_grad = weight_grad(up_delta, x_all)
+    routes = lax.all_to_all(route, "expert", split_axis=0, concat_axis=0, tiled=True)
+    per_expert = routes.transpose(1, 0, 2).reshape(rows, experts)
+    route_grad = jnp.sum(jnp.where(hit, per_expert[:, None, :], 0.0), axis=2)
+    return (mixed, token_grad, route_grad, gate_grad, up_grad, down_grad)
+
+
 def solution(mesh):
     placed = (
         P(("groups", "expert", "dp", "sub"), None),
@@ -145,8 +195,9 @@
         P(("expert", "dp"), "sub", None),
         P(("expert", "dp"), "sub", None),
     )
+    body = shards_dense if mesh.shape["dp"] <= 2 else shards
     return jax.shard_map(
-        shards,
+        body,
         mesh=mesh,
         in_specs=placed,
         out_specs=(

time: 187 us -> 384 us (2.05)
  waiting for transfers between devices: 87.8 us -> 313 us
  local copies, waits for them, and re-layouts: 29.2 us -> 6.32 us
  starting transfers between devices: 23 us -> 4.96 us
  blocking collectives: 0 us -> 11.9 us
  matrix products: 21.5 us -> 31.3 us
  other arithmetic: 10.5 us -> 2.19 us
    reduce_scatter x3 -> x5, waiting for transfers between devices: 0.01 us -> 160 us  [the longest x3 108 us: weight_grad(): lax.psum_scatter(part, ('dp', 'sub'), scatter_dimension=0, tiled=True)[None]]
    all_gather x3 -> x5, waiting for transfers between devices: 8.48 us -> 144 us  [the longest x1 38.8 us: shards_dense(): x_all = lax.all_gather(tokens, 'expert', axis=0, tiled=True)]
    all_to_all x5 -> x1, waiting for transfers between devices: 77.2 us -> 5.56 us  [shards_dense(): lax.all_to_all(route, 'expert', split_axis=0, concat_axis=0, tiled=True)]
    all_to_all x5 -> x1, starting transfers between devices: 22.6 us -> 4.6 us  [shards_dense(): lax.all_to_all(route, 'expert', split_axis=0, concat_axis=0, tiled=True)]
    all_gather x0 -> x1, blocking collectives: none -> 11.9 us  [shards_dense(): w_all = lax.all_gather(by_expert, 'expert', axis=0, tiled=True)]
    dot_general x9, matrix products: 21.5 us -> 31.3 us  [the longest x3 9.96 us: weight_grad(): jnp.einsum('rf,rd->fd', left, right, preferred_element_type=f32)]
    scatter x3 -> x0, local copies, waits for them, and re-layouts: 8.05 us -> none  [the longest x1 2.95 us: shards(): send_x = jnp.zeros((rows_total, features), jnp.bfloat16).at[target].set(j...]
    reduce_sum x4 -> x2, other arithmetic: 7.62 us -> 1.2 us  [the longest x1 0.62 us: shards_dense(): jnp.sum((hidden * back).reshape(stages, rows, dp, units // dp), axis=3)]
  transfers between devices with their start and end apart: 11 -> 11, of which waited for: 6 -> 11; matrix products, arithmetic and copies ran while one was open for 26% -> 6% of each run, Pallas kernels for 0% -> 0%
where the time goes in v1:
time: 384 us
  waiting for transfers between devices  313 us (82%)
  matrix products  31.3 us (8%)
  between operations  14.3 us (4%)
  blocking collectives  11.9 us (3%)
  local copies, waits for them, and re-layouts  6.32 us (2%)
  starting transfers between devices  4.96 us (1%)
    reduce_scatter x3, waiting for transfers between devices, weight_grad(): lax.psum_scatter(part, ('dp', 'sub'), scatter_dimension=0, tiled=True)[None]  108 us
    all_gather x1, waiting for transfers between devices, shards_dense(): x_all = lax.all_gather(tokens, 'expert', axis=0, tiled=True)  38.8 us
    reduce_scatter x1, waiting for transfers between devices, shards_dense(): lax.psum_scatter(token_part, 'expert', scatter_dimension=0, tiled=True)  37.2 us
    all_gather x1, waiting for transfers between devices, shards_dense(): dy_all = lax.all_gather(out_grad, 'expert', axis=0, tiled=True)  34.3 us
    all_gather x1, waiting for transfers between devices, shards_dense(): up_w = lax.all_gather(up_weight[0], ('dp', 'sub'), axis=0, tiled=True)  24.5 us
    all_gather x1, waiting for transfers between devices, shards_dense(): down_w = lax.all_gather(down_weight[0], ('dp', 'sub'), axis=0, tiled=True)  24.4 us
    all_gather x1, waiting for transfers between devices, shards_dense(): gate_w = lax.all_gather(gate_weight[0], ('dp', 'sub'), axis=0, tiled=True)  22.1 us
    reduce_scatter x1, waiting for transfers between devices, shards_dense(): lax.psum_scatter(mixed_part, 'expert', scatter_dimension=0, tiled=True)  15.6 us
  transfers between devices with their start and end apart: 11, of which 11 were waited for; matrix products, arithmetic and copies ran while one was open for 6% of the time, Pallas kernels for 0%

profile of v1, /device:TPU:0, one launch (start us, length us, event | category | flops | bytes accessed | tf_op | source)
XLA Modules:
  0.0 384.1 jit_solution(7755519864015469815)
XLA Ops:
  7.2 0.7 all-gather.9.cloned.1.call-update
  7.9 0.7 all-gather.15.cloned.1.call-update
  8.7 0.7 all-gather.13.cloned.1.call-update
  10.5 38.8 %all-gather.9.cloned.1.call-done = bf16[512,1536]{1,0:T(8,128)(2,1)} async-done(((bf16[128,1536]{1,0:T(8,128)(2,1)}), bf16[512,1536]{1,0:T(8,128)(2,1)}) %all-gather.9.cloned.1.call-update) | async-done | bytes 1572880 | tf_op jit(solution)/shard_map/all_gather | solution.py:149
  49.4 24.5 %all-gather.15.cloned.1.call-done = bf16[1,768,1536]{2,1,0:T(8,128)(2,1)} async-done(((bf16[1,192,1536]{2,1,0:T(8,128)(2,1)}), bf16[1,768,1536]{2,1,0:T(8,128)(2,1)}) %all-gather.15.cloned.1.call-update) | async-done | bytes 2359312 | tf_op jit(solution)/shard_map/all_gather | solution.py:151
  73.9 3.6 fusion.5
  77.5 22.1 %all-gather.13.cloned.1.call-done = bf16[1,768,1536]{2,1,0:T(8,128)(2,1)} async-done(((bf16[1,192,1536]{2,1,0:T(8,128)(2,1)}), bf16[1,768,1536]{2,1,0:T(8,128)(2,1)}) %all-gather.13.cloned.1.call-update) | async-done | bytes 2359312 | tf_op jit(solution)/shard_map/all_gather | solution.py:150
  99.6 4.2 %fusion.9 = f32[512,768]{1,0:T(8,128)} fusion(bf16[512,1536]{1,0:T(8,128)(2,1)S(1)} %copy-done.7, bf16[1,768,1536]{2,1,0:T(8,128)(2,1)} %all-gather.13.cloned.1.call-done), kind=kOutput, calls=%fused_computation.14 | convolution fusion | flops 1207959552 | bytes 5505024 | tf_op jit(solution)/shard_map/rd,fd->rf/dot_general | solution.py:157
  103.8 34.3 %all-gather.11.cloned.1.call-done = bf16[512,1536]{1,0:T(8,128)(2,1)} async-done(((bf16[128,1536]{1,0:T(8,128)(2,1)}), bf16[512,1536]{1,0:T(8,128)(2,1)}) %all-gather.11.cloned.1.call-update) | async-done | bytes 1572880 | tf_op jit(solution)/shard_map/all_gather | solution.py:153
  138.1 24.4 %all-gather.17.cloned.1.call-done = bf16[1,768,1536]{2,1,0:T(8,128)(2,1)} async-done(((bf16[1,192,1536]{2,1,0:T(8,128)(2,1)}), bf16[1,768,1536]{2,1,0:T(8,128)(2,1)}) %all-gather.17.cloned.1.call-update) | async-done | bytes 2359312 | tf_op jit(solution)/shard_map/all_gather | solution.py:152
  162.5 5.2 %fusion.11 = (f32[512,768]{1,0:T(8,128)S(1)}, f32[512,768]{1,0:T(8,128)}) fusion(f32[512,768]{1,0:T(8,128)S(1)} %fusion.5, f32[512,768]{1,0:T(8,128)} %fusion.9, bf16[512,1536]{1,0:T(8,128)(2,1)} %all-gather.11.cloned.1.call-done, bf16[1,768,1536]{2,1,0:T(8,128)(2,1)} %all-gather.17.cloned.1.call-done), kind=kOutput, calls=%fused_computation.25 | convolution fusion | flops 1210318848 | bytes 10223616 | tf_op jit(solution)/shard_map/rd,fd->rf/dot_general | solution.py:164
  167.7 0.8 reshape.22
  169.2 0.7 copy.27
  169.9 4.6 %all-to-all-start = ((f32[4,128,2]{1,2,0:T(2,128)}), f32[4,128,2]{1,2,0:T(2,128)S(1)}, u32[]{:S(2)}, u32[]{:S(2)}) async-start(f32[4,128,2]{1,2,0:T(2,128)} %copy.27), calls=%async_computation.2 | async-start | bytes 8192 | tf_op jit(solution)/shard_map/all_to_all | solution.py:182
  174.5 5.6 %all-to-all-done = f32[4,128,2]{1,2,0:T(2,128)S(1)} async-done(((f32[4,128,2]{1,2,0:T(2,128)}), f32[4,128,2]{1,2,0:T(2,128)S(1)}, u32[]{:S(2)}, u32[]{:S(2)}) %all-to-all-start) | async-done | bytes 4128 | tf_op jit(solution)/shard_map/all_to_all | solution.py:182
  180.7 11.9 %all_gather.18 = bf16[512,8]{0,1:T(8,128)(2,1)S(1)} all-gather(bf16[128,8]{0,1:T(8,128)(2,1)S(1)} %get-tuple-element.7), channel_id=1, replica_groups=mesh['groups'=2,'expert'=4,'dp'=2,'sub'=2] {'expert'}, dimensions={0}, use_global_device_ids=true | all-gather | bytes 10240 | tf_op jit(solution)/shard_map/all_gather | solution.py:148
  193.5 0.7 copy-done.3
  194.1 0.7 copy-done.1
  195.3 1.0 multiply_convert_fusion
  196.3 0.7 copy-done.6
  197.0 2.5 convolution_convert_fusion.3
  199.6 3.2 fusion.7
  202.8 2.6 fusion
  205.5 4.3 %convolution_convert_fusion = bf16[768,1536]{1,0:T(8,128)(2,1)} fusion(bf16[512,768]{1,0:T(8,128)(2,1)S(1)} %get-tuple-element.10, bf16[512,1536]{1,0:T(8,128)(2,1)} %all-gather.11.cloned.1.call-done), kind=kOutput, calls=%fused_computation | convolution fusion | flops 1209139200 | bytes 4718592 | tf_op jit(solution)/shard_map/rf,rd->fd/dot_general | solution.py:176
  209.8 1.3 copy-done.8
  211.2 2.8 convolution_convert_fusion.2
  214.1 2.9 convolution_convert_fusion.1
  217.0 15.6 %reduce-scatter.6.cloned.1.call-done = bf16[128,1536]{1,0:T(8,128)(2,1)} async-done(((bf16[512,1536]{1,0:T(8,128)(2,1)}), bf16[128,1536]{1,0:T(8,128)(2,1)}) %reduce-scatter.6.cloned.1.call-update) | async-done | bytes 393232 | tf_op jit(solution)/shard_map/reduce_scatter | solution.py:163
  232.6 37.2 %reduce-scatter.8.cloned.1.call-done = bf16[128,1536]{1,0:T(8,128)(2,1)} async-done(((bf16[512,1536]{1,0:T(8,128)(2,1)}), bf16[128,1536]{1,0:T(8,128)(2,1)}) %reduce-scatter.8.cloned.1.call-update) | async-done | bytes 393232 | tf_op jit(solution)/shard_map/reduce_scatter | solution.py:173
  269.8 35.1 %reduce-scatter.14.cloned.1.call-done = bf16[192,1536]{1,0:T(8,128)(2,1)} async-done(((bf16[768,1536]{1,0:T(8,128)(2,1)}), bf16[192,1536]{1,0:T(8,128)(2,1)}) %reduce-scatter.14.cloned.1.call-update) | async-done | bytes 589840 | tf_op jit(solution)/shard_map/reduce_scatter | solution.py:177
  304.9 36.4 %reduce-scatter.10.cloned.1.call-done = bf16[192,1536]{1,0:T(8,128)(2,1)} async-done(((bf16[768,1536]{1,0:T(8,128)(2,1)}), bf16[192,1536]{1,0:T(8,128)(2,1)}) %reduce-scatter.10.cloned.1.call-update) | async-done | bytes 589840 | tf_op jit(solution)/shard_map/reduce_scatter | solution.py:177
  341.3 36.0 %reduce-scatter.12.cloned.1.call-done = bf16[192,1536]{1,0:T(8,128)(2,1)} async-done(((bf16[768,1536]{1,0:T(8,128)(2,1)}), bf16[192,1536]{1,0:T(8,128)(2,1)}) %reduce-scatter.12.cloned.1.call-update) | async-done | bytes 589840 | tf_op jit(solution)/shard_map/reduce_scatter | solution.py:177
  (40 shorter events, 4.1 us)
Async XLA Ops:
  7.2 42.2 %all-gather.9.cloned.1.call-start = ((), (), s32[]{:S(2)}) async-start(), calls=%async_computation.6 | async-start | bytes 1966080 | tf_op jit(solution)/shard_map/all_gather | solution.py:149
  7.9 66.0 %all-gather.15.cloned.1.call-start = ((), (), s32[]{:S(2)}) async-start(), calls=%async_computation.14 | async-start | bytes 2949120 | tf_op jit(solution)/shard_map/all_gather | solution.py:151
  8.6 90.9 %all-gather.13.cloned.1.call-start = ((), (), s32[]{:S(2)}) async-start(), calls=%async_computation.13 | async-start | bytes 2949120 | tf_op jit(solution)/shard_map/all_gather | solution.py:150
  9.4 128.8 %all-gather.11.cloned.1.call-start = ((), (), s32[]{:S(2)}) async-start(), calls=%async_computation.8 | async-start | bytes 1966080 | tf_op jit(solution)/shard_map/all_gather | solution.py:153
  10.0 152.6 %all-gather.17.cloned.1.call-start = ((), (), s32[]{:S(2)}) async-start(), calls=%async_computation.15 | async-start | bytes 2949120 | tf_op jit(solution)/shard_map/all_gather | solution.py:152
  49.4 50.2 %copy-start.7 = (bf16[512,1536]{1,0:T(8,128)(2,1)S(1)}, bf16[512,1536]{1,0:T(8,128)(2,1)}, u32[]{:S(2)}) copy-start(bf16[512,1536]{1,0:T(8,128)(2,1)} %all-gather.9.cloned.1.call-done) | copy-start | bytes 4718596
  77.5 85.0 %copy-start = (f32[512,768]{1,0:T(8,128)}, f32[512,768]{1,0:T(8,128)S(1)}, u32[]{:S(2)}) copy-start(f32[512,768]{1,0:T(8,128)S(1)} %fusion.5) | copy-start | bytes 4718596
  168.6 6.0 %copy-start.9 = (bf16[128,2]{0,1:T(2,128)(2,1)S(1)}, bf16[128,2]{0,1:T(2,128)(2,1)}, u32[]{:S(2)}) copy-start(bf16[128,2]{0,1:T(2,128)(2,1)} %param.9) | copy-start | bytes 1540
  168.6 11.5 %copy-start.4 = (s32[128,2]{0,1:T(2,128)S(1)}, s32[128,2]{0,1:T(2,128)}, u32[]{:S(2)}) copy-start(s32[128,2]{0,1:T(2,128)} %param.8) | copy-start | bytes 3076
  169.9 10.2 %all-to-all-start = ((f32[4,128,2]{1,2,0:T(2,128)}), f32[4,128,2]{1,2,0:T(2,128)S(1)}, u32[]{:S(2)}, u32[]{:S(2)}) async-start(f32[4,128,2]{1,2,0:T(2,128)} %copy.27), calls=%async_computation.2 | async-start | bytes 8192 | tf_op jit(solution)/shard_map/all_to_all | solution.py:182
  174.5 58.1 %reduce-scatter.6.cloned.1.call-start = ((), (), s32[]{:S(2)}) async-start(), calls=%async_computation.7 | async-start | bytes 1966080 | tf_op jit(solution)/shard_map/reduce_scatter | solution.py:163
  192.7 1.4 copy-start.3
  193.3 1.5 copy-start.1
  193.3 2.0 copy-start.2
  195.3 1.7 copy-start.6
  199.5 70.2 %reduce-scatter.8.cloned.1.call-start = ((), (), s32[]{:S(2)}) async-start(), calls=%async_computation.9 | async-start | bytes 1966080 | tf_op jit(solution)/shard_map/reduce_scatter | solution.py:173
  199.6 3.2 copy-start.5
  205.5 99.4 %reduce-scatter.14.cloned.1.call-start = ((), (), s32[]{:S(2)}) async-start(), calls=%async_computation.12 | async-start | bytes 2949120 | tf_op jit(solution)/shard_map/reduce_scatter | solution.py:177
  209.8 1.4 copy-start.8
  209.8 131.5 %reduce-scatter.10.cloned.1.call-start = ((), (), s32[]{:S(2)}) async-start(), calls=%async_computation.10 | async-start | bytes 2949120 | tf_op jit(solution)/shard_map/reduce_scatter | solution.py:177
  214.0 163.3 %reduce-scatter.12.cloned.1.call-start = ((), (), s32[]{:S(2)}) async-start(), calls=%async_computation.11 | async-start | bytes 2949120 | tf_op jit(solution)/shard_map/reduce_scatter | solution.py:177
Sparse Core Ops, SparseCore 0:
  9.6 39.7 all-gather.8
  50.9 22.9 all-gather.14
  75.5 24.0 all-gather.12
  101.0 37.0 all-gather.10
  139.5 22.9 all-gather.16
  199.7 32.8 reduce-scatter.5
  235.5 34.2 reduce-scatter.7
  272.9 31.9 reduce-scatter.13
  308.2 33.0 reduce-scatter.9
  344.2 33.0 reduce-scatter.11

commit v2 on v0

v2 whole, which is shorter than its diff:
```python
import jax
import jax.numpy as jnp
from jax import lax
from jax.sharding import PartitionSpec as P


def shards(tokens, expert_ids, route_weights, out_grad, gate_weight, up_weight, down_weight):
    f32, bf16 = jnp.float32, jnp.bfloat16
    tok_rows, features = tokens.shape
    top_count = expert_ids.shape[1]
    experts = lax.axis_size("expert") * lax.axis_size("dp")
    capacity = max(2, 3 * tok_rows * top_count // (2 * experts))
    rows_total = experts * capacity

    hit = expert_ids[:, :, None] == jnp.arange(experts, dtype=jnp.int32)[None, None, :]
    named = jnp.any(hit, axis=1).astype(bf16)
    row = jnp.arange(tok_rows)
    earlier = (row[:, None] > row[None, :]).astype(bf16)
    before = jnp.dot(earlier, named, preferred_element_type=f32)
    slot_index = jnp.sum(jnp.where(hit, before[:, None, :], 0.0), axis=2).astype(jnp.int32)
    target = expert_ids * capacity + slot_index
    slots = jnp.arange(rows_total, dtype=jnp.int32)
    picks = target.T[:, :, None] == slots[None, None, :]
    pick = picks.astype(bf16)
    place = jnp.any(picks, axis=0).astype(bf16)
    weigh = jnp.sum(
        jnp.where(picks, route_weights.T.astype(f32)[:, :, None], 0.0), axis=0
    ).astype(bf16)

    def exchange(rows):
        moved = lax.all_to_all(
            rows.reshape(experts, capacity, features),
            ("expert", "dp"),
            split_axis=0,
            concat_axis=0,
            tiled=True,
        )
        return moved.reshape(rows_total, features)

    send_x = jnp.einsum("ts,td->sd", place, tokens, preferred_element_type=f32).astype(bf16)
    recv_x = exchange(send_x)
    send_dy = jnp.einsum("ts,td->sd", weigh, out_grad, preferred_element_type=f32).astype(bf16)
    recv_dy = exchange(send_dy)
    gate_full = lax.all_gather(gate_weight[0], "sub", axis=0, tiled=True)
    up_full = lax.all_gather(up_weight[0], "sub", axis=0, tiled=True)
    down_full = lax.all_gather(down_weight[0], "sub", axis=0, tiled=True)

    gate = jnp.einsum("rd,fd->rf", recv_x, gate_full, preferred_element_type=f32)
    up = jnp.einsum("rd,fd->rf", recv_x, up_full, preferred_element_type=f32)
    sigmoid = jax.nn.sigmoid(gate)
    hidden = (gate * sigmoid * up).astype(bf16)
    output = jnp.einsum("rf,fd->rd", hidden, down_full, preferred_element_type=f32).astype(bf16)
    back_out = exchange(output)

    hidden_grad = jnp.einsum("rd,fd->rf", recv_dy, down_full, preferred_element_type=f32)
    gate_delta = (hidden_grad * up * sigmoid * (1.0 + gate * (1.0 - sigmoid))).astype(bf16)
    up_delta = (hidden_grad * gate * sigmoid).astype(bf16)
    input_grad = (
        jnp.einsum("rf,fd->rd", gate_delta, gate_full, preferred_element_type=f32)
        + jnp.einsum("rf,fd->rd", up_delta, up_full, preferred_element_type=f32)
    ).astype(bf16)
    back_grad = exchange(input_grad)

    def weight_grad(left, right):
        part = jnp.einsum("rf,rd->fd", left, right, preferred_element_type=f32).astype(bf16)
        return lax.psum_scatter(part, "sub", scatter_dimension=0, tiled=True)[None]

    down_grad = weight_grad(hidden, recv_dy)
    gate_grad = weight_grad(gate_delta, recv_x)
    up_grad = weight_grad(up_delta, recv_x)

    weights = route_weights.astype(f32)
    cotangent = out_grad.astype(f32)
    visit = [jnp.dot(pick[k], back_out, preferred_element_type=f32) for k in range(top_count)]
    mixed = sum(weights[:, k : k + 1] * visit[k] for k in range(top_count)).astype(bf16)
    route_grad = jnp.stack([jnp.sum(cotangent * v, axis=1) for v in visit], axis=1)
    token_grad = jnp.einsum("ts,sd->td", place, back_grad, preferred_element_type=f32).astype(bf16)
    return (mixed, token_grad, route_grad, gate_grad, up_grad, down_grad)


def solution(mesh):
    rows = P(("groups", "expert", "dp", "sub"), None)
    weight = P(("expert", "dp"), "sub", None)
    grad = P(("groups", "expert", "dp"), "sub", None)
    return jax.shard_map(
        shards,
        mesh=mesh,
        in_specs=(rows,) * 4 + (weight,) * 3,
        out_specs=(rows,) * 3 + (grad,) * 3,
        check_vma=False,
    )
```

time: 187 us -> 166 us (0.89)
  local copies, waits for them, and re-layouts: 29.2 us -> 2.88 us
  waiting for transfers between devices: 87.8 us -> 99 us
  other arithmetic: 10.5 us -> 3.65 us
  matrix products: 21.5 us -> 27.3 us
  starting transfers between devices: 23 us -> 18.5 us
    all_to_all x5 -> x4, waiting for transfers between devices: 77.2 us -> 90.4 us  [exchange(): lax.all_to_all(rows.reshape(experts, capacity, features), ('expert', 'dp'...]
    scatter x3 -> x0, local copies, waits for them, and re-layouts: 8.05 us -> none  [the longest x1 2.95 us: shards(): send_x = jnp.zeros((rows_total, features), jnp.bfloat16).at[target].set(j...]
    reduce_sum x4 -> x2, other arithmetic: 7.62 us -> 0.85 us  [the longest x1 0.72 us: shards(): jnp.sum(jnp.where(hit, before[:, None, :], 0.0), axis=2).astype(jnp.int32)]
    broadcast_in_dim x4 -> x0, local copies, waits for them, and re-layouts: 6.53 us -> none  [the longest x3 5.13 us: shards(): jnp.repeat(out_grad, top_count, axis=0)]
    dot_general x9 -> x15, matrix products: 21.5 us -> 27.3 us  [the longest x3 5.52 us: weight_grad(): jnp.einsum('rf,rd->fd', left, right, preferred_element_type=f32)]
    gather x3 -> x0, local copies, waits for them, and re-layouts: 5.6 us -> none  [the longest x2 4.33 us: shards(): back_grad = returned[1].reshape(rows_total, features)[target]]
    all_to_all x5 -> x4, starting transfers between devices: 22.6 us -> 18.3 us  [exchange(): lax.all_to_all(rows.reshape(experts, capacity, features), ('expert', 'dp'...]
    convert_element_type x3 -> x0, local copies, waits for them, and re-layouts: 2.32 us -> none  [the longest x1 2.12 us: shards(): back_out.astype(jnp.float32)]
  transfers between devices with their start and end apart: 11 -> 10, of which waited for: 6 -> 5; matrix products, arithmetic and copies ran while one was open for 26% -> 13% of each run, Pallas kernels for 0% -> 0%
where the time goes in v2:
time: 166 us
  waiting for transfers between devices  99 us (60%)
  matrix products  27.3 us (16%)
  starting transfers between devices  18.5 us (11%)
  between operations  14.2 us (9%)
  other arithmetic  3.65 us (2%)
  local copies, waits for them, and re-layouts  2.88 us (2%)
    all_to_all x4, waiting for transfers between devices, exchange(): lax.all_to_all(rows.reshape(experts, capacity, features), ('expert', 'dp'...  90.4 us
    all_to_all x4, starting transfers between devices, exchange(): lax.all_to_all(rows.reshape(experts, capacity, features), ('expert', 'dp'...  18.3 us
    all_gather x1, waiting for transfers between devices, shards(): down_full = lax.all_gather(down_weight[0], 'sub', axis=0, tiled=True)  6.5 us
    dot_general x3, matrix products, weight_grad(): jnp.einsum('rf,rd->fd', left, right, preferred_element_type=f32)  5.52 us
  transfers between devices with their start and end apart: 10, of which 5 were waited for; matrix products, arithmetic and copies ran while one was open for 13% of the time, Pallas kernels for 0%

profile of v2, /device:TPU:0, one launch (start us, length us, event | category | flops | bytes accessed | tf_op | source)
XLA Modules:
  0.0 165.6 jit_solution(7950410422562510454)
XLA Ops:
  7.2 0.7 fusion.18
  8.1 0.7 select_reduce_fusion.1
  8.8 0.7 add_bitcast_fusion
  9.5 0.8 iota_compare_fusion
  10.3 1.5 convolution_convert_fusion.1
  11.8 7.3 %all-to-all-start = ((bf16[8,48,1536]{2,1,0:T(8,128)(2,1)}), bf16[8,48,1536]{2,1,0:T(8,128)(2,1)S(1)}, u32[]{:S(2)}, u32[]{:S(2)}) async-start(bf16[8,48,1536]{2,1,0:T(8,128)(2,1)} %bitcast.3), calls=%async_computation | async-start | bytes 2359296 | tf_op jit(solution)/shard_map/all_to_all | solution.py:31
  19.1 0.7 all-gather.9.cloned.1.call-update
  19.9 0.7 all-gather.7.cloned.1.call-update
  20.7 1.5 convolution_convert_fusion
  22.3 25.4 %all-to-all-done = bf16[8,48,1536]{2,1,0:T(8,128)(2,1)S(1)} async-done(((bf16[8,48,1536]{2,1,0:T(8,128)(2,1)}), bf16[8,48,1536]{2,1,0:T(8,128)(2,1)S(1)}, u32[]{:S(2)}, u32[]{:S(2)}) %all-to-all-start) | async-done | bytes 1179680 | tf_op jit(solution)/shard_map/all_to_all | solution.py:31
  47.6 3.6 %all-to-all-start.2 = ((bf16[8,48,1536]{2,1,0:T(8,128)(2,1)}), bf16[8,48,1536]{2,1,0:T(8,128)(2,1)S(1)}, u32[]{:S(2)}, u32[]{:S(2)}) async-start(bf16[8,48,1536]{2,1,0:T(8,128)(2,1)} %bitcast.13), calls=%async_computation.2 | async-start | bytes 2359296 | tf_op jit(solution)/shard_map/all_to_all | solution.py:31
  51.3 0.7 all-gather.11.cloned.1.call-update
  52.1 2.9 %fusion.5 = f32[384,384]{1,0:T(8,128)} fusion(bf16[384,1536]{1,0:T(8,128)(2,1)S(1)} %bitcast.69, bf16[1,384,1536]{2,1,0:T(8,128)(2,1)} %all-gather.9.cloned.1.call-done), kind=kOutput, calls=%fused_computation.13 | convolution fusion | flops 452984832 | bytes 2949120 | tf_op jit(solution)/shard_map/rd,fd->rf/dot_general | solution.py:49
  55.0 2.9 %fusion.9 = f32[384,384]{1,0:T(8,128)} fusion(bf16[384,1536]{1,0:T(8,128)(2,1)S(1)} %bitcast.70, bf16[1,384,1536]{2,1,0:T(8,128)(2,1)} %all-gather.7.cloned.1.call-done), kind=kOutput, calls=%fused_computation.17 | convolution fusion | flops 452984832 | bytes 2949120 | tf_op jit(solution)/shard_map/rd,fd->rf/dot_general | solution.py:48
  57.8 6.5 %all-gather.11.cloned.1.call-done = bf16[1,384,1536]{2,1,0:T(8,128)(2,1)} async-done(((bf16[1,192,1536]{2,1,0:T(8,128)(2,1)}), bf16[1,384,1536]{2,1,0:T(8,128)(2,1)}) %all-gather.11.cloned.1.call-update) | async-done | bytes 1179664 | tf_op jit(solution)/shard_map/all_gather | solution.py:46
  64.3 15.7 %all-to-all-done.2 = bf16[8,48,1536]{2,1,0:T(8,128)(2,1)S(1)} async-done(((bf16[8,48,1536]{2,1,0:T(8,128)(2,1)}), bf16[8,48,1536]{2,1,0:T(8,128)(2,1)S(1)}, u32[]{:S(2)}, u32[]{:S(2)}) %all-to-all-start.2) | async-done | bytes 1179680 | tf_op jit(solution)/shard_map/all_to_all | solution.py:31
  80.0 3.2 %multiply_convert_fusion = (bf16[384,384]{1,0:T(8,128)(2,1)S(1)}, bf16[384,384]{1,0:T(8,128)(2,1)}, bf16[384,384]{1,0:T(8,128)(2,1)S(1)}) fusion(f32[384,384]{1,0:T(8,128)} %fusion.9, f32[384,384]{1,0:T(8,128)} %fusion.5, bf16[384,1536]{1,0:T(8,128)(2,1)S(1)} %bitcast.74, bf16[1,384,1536]{2,1,0:T(8,128)(2,1)} %all-gather.11.cloned.1.call-done), kind=kOutput, calls=%fused_computation.24 | convolution fusion | flops 455344128 | bytes 4423680 | tf_op jit(solution)/shard_map/rd,fd->rf/dot_general | solution.py:55
  83.3 0.7 copy-done.4
  84.0 1.8 %convolution_convert_fusion.2 = bf16[384,1536]{1,0:T(8,128)(2,1)} fusion(bf16[384,384]{1,0:T(8,128)(2,1)S(1)} %get-tuple-element.11, bf16[384,1536]{1,0:T(8,128)(2,1)S(1)} %bitcast.75), kind=kOutput, calls=%fused_computation.4 | convolution fusion | flops 453574656 | bytes 2654208 | tf_op jit(solution)/shard_map/rf,rd->fd/dot_general | solution.py:65
  85.9 0.9 copy-done.5
  86.8 1.8 %convolution_convert_fusion.4 = bf16[384,1536]{1,0:T(8,128)(2,1)} fusion(bf16[384,384]{1,0:T(8,128)(2,1)S(1)} %copy-done.5, bf16[384,1536]{1,0:T(8,128)(2,1)S(1)} %bitcast.71), kind=kOutput, calls=%fused_computation.6 | convolution fusion | flops 453574656 | bytes 2654208 | tf_op jit(solution)/shard_map/rf,rd->fd/dot_general | solution.py:65
  88.6 1.2 copy-done.3
  89.9 2.8 %convolution_convert_fusion.5 = bf16[384,1536]{1,0:T(8,128)(2,1)} fusion(bf16[384,384]{1,0:T(8,128)(2,1)} %copy-done.4, bf16[1,384,1536]{2,1,0:T(8,128)(2,1)S(1)} %copy-done.3), kind=kOutput, calls=%fused_computation.7 | convolution fusion | flops 453574656 | bytes 2654208 | tf_op jit(solution)/shard_map/rf,fd->rd/dot_general | solution.py:52
  92.7 3.6 %all-to-all-start.1 = ((bf16[8,48,1536]{2,1,0:T(8,128)(2,1)}), bf16[8,48,1536]{2,1,0:T(8,128)(2,1)S(1)}, u32[]{:S(2)}, u32[]{:S(2)}) async-start(bf16[8,48,1536]{2,1,0:T(8,128)(2,1)} %bitcast.76), calls=%async_computation.1 | async-start | bytes 2359296 | tf_op jit(solution)/shard_map/all_to_all | solution.py:31
  96.4 1.9 %convolution_convert_fusion.3 = bf16[384,1536]{1,0:T(8,128)(2,1)} fusion(bf16[384,384]{1,0:T(8,128)(2,1)S(1)} %get-tuple-element.9, bf16[384,1536]{1,0:T(8,128)(2,1)S(1)} %bitcast.72), kind=kOutput, calls=%fused_computation.5 | convolution fusion | flops 453574656 | bytes 2654208 | tf_op jit(solution)/shard_map/rf,rd->fd/dot_general | solution.py:65
  98.3 2.2 %fusion.7 = f32[384,1536]{1,0:T(8,128)S(1)} fusion(bf16[384,384]{1,0:T(8,128)(2,1)} %get-tuple-element.10, bf16[1,384,1536]{2,1,0:T(8,128)(2,1)} %all-gather.7.cloned.1.call-done), kind=kOutput, calls=%fused_computation.15 | convolution fusion | flops 452984832 | bytes 3833856 | tf_op jit(solution)/shard_map/rf,fd->rd/dot_general | solution.py:59
  100.5 1.8 %fusion = bf16[384,1536]{1,0:T(8,128)(2,1)} fusion(f32[384,1536]{1,0:T(8,128)S(1)} %fusion.7, bf16[384,384]{1,0:T(8,128)(2,1)S(1)} %get-tuple-element.9, bf16[1,384,1536]{2,1,0:T(8,128)(2,1)S(1)} %copy-done.2), kind=kOutput, calls=%fused_computation.1 | convolution fusion | flops 454164480 | bytes 5013504 | tf_op jit(solution)/shard_map/rf,fd->rd/dot_general | solution.py:60
  102.3 22.7 %all-to-all-done.1 = bf16[8,48,1536]{2,1,0:T(8,128)(2,1)S(1)} async-done(((bf16[8,48,1536]{2,1,0:T(8,128)(2,1)}), bf16[8,48,1536]{2,1,0:T(8,128)(2,1)S(1)}, u32[]{:S(2)}, u32[]{:S(2)}) %all-to-all-start.1) | async-done | bytes 1179680 | tf_op jit(solution)/shard_map/all_to_all | solution.py:31
  125.1 3.8 %all-to-all-start.3 = ((bf16[8,48,1536]{2,1,0:T(8,128)(2,1)}), bf16[8,48,1536]{2,1,0:T(8,128)(2,1)S(1)}, u32[]{:S(2)}, u32[]{:S(2)}) async-start(bf16[8,48,1536]{2,1,0:T(8,128)(2,1)} %bitcast.15), calls=%async_computation.3 | async-start | bytes 2359296 | tf_op jit(solution)/shard_map/all_to_all | solution.py:31
  129.3 1.2 fusion.11
  131.0 26.6 %all-to-all-done.3 = bf16[8,48,1536]{2,1,0:T(8,128)(2,1)S(1)} async-done(((bf16[8,48,1536]{2,1,0:T(8,128)(2,1)}), bf16[8,48,1536]{2,1,0:T(8,128)(2,1)S(1)}, u32[]{:S(2)}, u32[]{:S(2)}) %all-to-all-start.3) | async-done | bytes 1179680 | tf_op jit(solution)/shard_map/all_to_all | solution.py:31
  157.6 1.1 convolution_convert_fusion.6
  (33 shorter events, 1.6 us)
Async XLA Ops:
  7.2 3.1 %copy-start = (bf16[128,1536]{1,0:T(8,128)(2,1)S(1)}, bf16[128,1536]{1,0:T(8,128)(2,1)}, u32[]{:S(2)}) copy-start(bf16[128,1536]{1,0:T(8,128)(2,1)} %param.7) | copy-start | bytes 1179652
  11.8 35.8 %all-to-all-start = ((bf16[8,48,1536]{2,1,0:T(8,128)(2,1)}), bf16[8,48,1536]{2,1,0:T(8,128)(2,1)S(1)}, u32[]{:S(2)}, u32[]{:S(2)}) async-start(bf16[8,48,1536]{2,1,0:T(8,128)(2,1)} %bitcast.3), calls=%async_computation | async-start | bytes 2359296 | tf_op jit(solution)/shard_map/all_to_all | solution.py:31
  19.1 1.5 copy-start.7
  19.1 1.7 %copy-start.1 = (bf16[128,1536]{1,0:T(8,128)(2,1)S(1)}, bf16[128,1536]{1,0:T(8,128)(2,1)}, u32[]{:S(2)}) copy-start(bf16[128,1536]{1,0:T(8,128)(2,1)} %param.10) | copy-start | bytes 1179652
  19.1 33.0 %all-gather.9.cloned.1.call-start = ((), (), s32[]{:S(2)}) async-start(), calls=%async_computation.11 | async-start | bytes 1769472 | tf_op jit(solution)/shard_map/all_gather | solution.py:45
  19.8 35.1 %all-gather.7.cloned.1.call-start = ((), (), s32[]{:S(2)}) async-start(), calls=%async_computation.10 | async-start | bytes 1769472 | tf_op jit(solution)/shard_map/all_gather | solution.py:44
  47.6 32.4 %all-to-all-start.2 = ((bf16[8,48,1536]{2,1,0:T(8,128)(2,1)}), bf16[8,48,1536]{2,1,0:T(8,128)(2,1)S(1)}, u32[]{:S(2)}, u32[]{:S(2)}) async-start(bf16[8,48,1536]{2,1,0:T(8,128)(2,1)} %bitcast.13), calls=%async_computation.2 | async-start | bytes 2359296 | tf_op jit(solution)/shard_map/all_to_all | solution.py:31
  51.3 13.1 %all-gather.11.cloned.1.call-start = ((), (), s32[]{:S(2)}) async-start(), calls=%async_computation.12 | async-start | bytes 1769472 | tf_op jit(solution)/shard_map/all_gather | solution.py:46
  52.0 106.7 %reduce-scatter.8.cloned.1.call-start = ((), (), s32[]{:S(2)}) async-start(), calls=%async_computation.9 | async-start | bytes 1769472 | tf_op jit(solution)/shard_map/reduce_scatter | solution.py:66
  83.3 0.7 copy-start.4
  85.8 1.0 copy-start.5
  85.8 72.9 %reduce-scatter.4.cloned.1.call-start = ((), (), s32[]{:S(2)}) async-start(), calls=%async_computation.7 | async-start | bytes 1769472 | tf_op jit(solution)/shard_map/reduce_scatter | solution.py:66
  88.6 1.3 copy-start.3
  92.7 32.4 %all-to-all-start.1 = ((bf16[8,48,1536]{2,1,0:T(8,128)(2,1)}), bf16[8,48,1536]{2,1,0:T(8,128)(2,1)S(1)}, u32[]{:S(2)}, u32[]{:S(2)}) async-start(bf16[8,48,1536]{2,1,0:T(8,128)(2,1)} %bitcast.76), calls=%async_computation.1 | async-start | bytes 2359296 | tf_op jit(solution)/shard_map/all_to_all | solution.py:31
  96.3 62.4 %reduce-scatter.6.cloned.1.call-start = ((), (), s32[]{:S(2)}) async-start(), calls=%async_computation.8 | async-start | bytes 1769472 | tf_op jit(solution)/shard_map/reduce_scatter | solution.py:66
  98.3 2.2 %copy-start.2 = (bf16[1,384,1536]{2,1,0:T(8,128)(2,1)S(1)}, bf16[1,384,1536]{2,1,0:T(8,128)(2,1)}, u32[]{:S(2)}) copy-start(bf16[1,384,1536]{2,1,0:T(8,128)(2,1)} %all-gather.9.cloned.1.call-done) | copy-start | bytes 3538948
  125.1 3.8 %copy-start.6 = (pred[2,128,384]{2,1,0:T(32,128)(4,1)S(1)}, pred[2,128,384]{2,1,0:T(32,128)(4,1)}, u32[]{:S(2)}) copy-start(pred[2,128,384]{2,1,0:T(32,128)(4,1)} %get-tuple-element.14) | copy-start | bytes 294916
  125.1 32.5 %all-to-all-start.3 = ((bf16[8,48,1536]{2,1,0:T(8,128)(2,1)}), bf16[8,48,1536]{2,1,0:T(8,128)(2,1)S(1)}, u32[]{:S(2)}, u32[]{:S(2)}) async-start(bf16[8,48,1536]{2,1,0:T(8,128)(2,1)} %bitcast.15), calls=%async_computation.3 | async-start | bytes 2359296 | tf_op jit(solution)/shard_map/all_to_all | solution.py:31
Sparse Core Ops, SparseCore 0:
  21.5 10.6 all-gather.8
  33.7 10.3 all-gather.6
  53.7 10.6 all-gather.10
  86.0 7.7 reduce-scatter.7
  96.5 9.8 reduce-scatter.3
  109.1 9.8 reduce-scatter.5

commit v3 on v2

--- a/solution.py
+++ b/solution.py
@@ -48,8 +48,9 @@
     gate = jnp.einsum("rd,fd->rf", recv_x, gate_full, preferred_element_type=f32)
     up = jnp.einsum("rd,fd->rf", recv_x, up_full, preferred_element_type=f32)
     sigmoid = jax.nn.sigmoid(gate)
-    hidden = (gate * sigmoid * up).astype(bf16)
+    hidden = lax.optimization_barrier((gate * sigmoid * up).astype(bf16))
     output = jnp.einsum("rf,fd->rd", hidden, down_full, preferred_element_type=f32).astype(bf16)
+    output, recv_dy = lax.optimization_barrier((output, recv_dy))
     back_out = exchange(output)
 
     hidden_grad = jnp.einsum("rd,fd->rf", recv_dy, down_full, preferred_element_type=f32)

time: 166 us -> 161 us (0.970)
  waiting for transfers between devices: 99 us -> 95.8 us
  local copies, waits for them, and re-layouts: 2.88 us -> 0.74 us
    all_to_all x4, waiting for transfers between devices: 90.4 us -> 87.3 us  [exchange(): lax.all_to_all(rows.reshape(experts, capacity, features), ('expert', 'dp'...]
    unnamed x16 -> x12, local copies, waits for them, and re-layouts: 2.87 us -> 0.74 us
  transfers between devices with their start and end apart: 10 -> 10, of which waited for: 5 -> 5; matrix products, arithmetic and copies ran while one was open for 13% -> 15% of each run, Pallas kernels for 0% -> 0%
where the time goes in v3:
time: 161 us; the launch traced here: 160 us
  waiting for transfers between devices  95.8 us (60%)
  matrix products  27 us (17%)
  starting transfers between devices  18.5 us (11%)
  between operations  14.2 us (9%)
  other arithmetic  3.65 us (2%)
    all_to_all x4, waiting for transfers between devices, exchange(): lax.all_to_all(rows.reshape(experts, capacity, features), ('expert', 'dp'...  87.3 us
    all_to_all x4, starting transfers between devices, exchange(): lax.all_to_all(rows.reshape(experts, capacity, features), ('expert', 'dp'...  18.3 us
    all_gather x1, waiting for transfers between devices, shards(): down_full = lax.all_gather(down_weight[0], 'sub', axis=0, tiled=True)  6.35 us
    dot_general x3, matrix products, weight_grad(): jnp.einsum('rf,rd->fd', left, right, preferred_element_type=f32)  5.57 us
  transfers between devices with their start and end apart: 10, of which 5 were waited for; matrix products, arithmetic and copies ran while one was open for 15% of the time, Pallas kernels for 0%

profile of v3, /device:TPU:0, one launch (start us, length us, event | category | flops | bytes accessed | tf_op | source)
XLA Modules:
  0.0 160.0 jit_solution(10908651152558807164)
XLA Ops:
  7.2 0.7 fusion.18
  8.1 0.7 select_reduce_fusion.1
  8.8 0.7 add_bitcast_fusion
  9.5 0.8 iota_compare_fusion
  10.3 1.6 convolution_convert_fusion.1
  11.8 7.3 %all-to-all-start = ((bf16[8,48,1536]{2,1,0:T(8,128)(2,1)}), bf16[8,48,1536]{2,1,0:T(8,128)(2,1)S(1)}, u32[]{:S(2)}, u32[]{:S(2)}) async-start(bf16[8,48,1536]{2,1,0:T(8,128)(2,1)} %bitcast.3), calls=%async_computation | async-start | bytes 2359296 | tf_op jit(solution)/shard_map/all_to_all | solution.py:31
  19.1 0.7 all-gather.7.cloned.1.call-update
  19.9 0.7 all-gather.9.cloned.1.call-update
  20.7 1.5 convolution_convert_fusion
  22.3 25.4 %all-to-all-done = bf16[8,48,1536]{2,1,0:T(8,128)(2,1)S(1)} async-done(((bf16[8,48,1536]{2,1,0:T(8,128)(2,1)}), bf16[8,48,1536]{2,1,0:T(8,128)(2,1)S(1)}, u32[]{:S(2)}, u32[]{:S(2)}) %all-to-all-start) | async-done | bytes 1179680 | tf_op jit(solution)/shard_map/all_to_all | solution.py:31
  47.6 3.6 %all-to-all-start.1 = ((bf16[8,48,1536]{2,1,0:T(8,128)(2,1)}), bf16[8,48,1536]{2,1,0:T(8,128)(2,1)S(1)}, u32[]{:S(2)}, u32[]{:S(2)}) async-start(bf16[8,48,1536]{2,1,0:T(8,128)(2,1)} %bitcast.9), calls=%async_computation.1 | async-start | bytes 2359296 | tf_op jit(solution)/shard_map/all_to_all | solution.py:31
  51.3 0.7 all-gather.11.cloned.1.call-update
  52.1 2.9 %fusion.9 = f32[384,384]{1,0:T(8,128)} fusion(bf16[384,1536]{1,0:T(8,128)(2,1)S(1)} %bitcast.71, bf16[1,384,1536]{2,1,0:T(8,128)(2,1)} %all-gather.7.cloned.1.call-done), kind=kOutput, calls=%fused_computation.17 | convolution fusion | flops 452984832 | bytes 2949120 | tf_op jit(solution)/shard_map/rd,fd->rf/dot_general | solution.py:48
  55.0 3.0 %multiply_convert_fusion.2 = (bf16[384,384]{1,0:T(8,128)(2,1)S(1)}, f32[384,384]{1,0:T(8,128)}) fusion(f32[384,384]{1,0:T(8,128)} %fusion.9, bf16[384,1536]{1,0:T(8,128)(2,1)S(1)} %bitcast.72, bf16[1,384,1536]{2,1,0:T(8,128)(2,1)} %all-gather.9.cloned.1.call-done), kind=kOutput, calls=%fused_computation.26 | convolution fusion | flops 453869568 | bytes 3833856 | tf_op jit(solution)/shard_map/rd,fd->rf/dot_general | solution.py:49
  58.0 6.3 %all-gather.11.cloned.1.call-done = bf16[1,384,1536]{2,1,0:T(8,128)(2,1)} async-done(((bf16[1,192,1536]{2,1,0:T(8,128)(2,1)}), bf16[1,384,1536]{2,1,0:T(8,128)(2,1)}) %all-gather.11.cloned.1.call-update) | async-done | bytes 1179664 | tf_op jit(solution)/shard_map/all_gather | solution.py:46
  64.4 3.1 %convolution_convert_fusion.5 = bf16[384,1536]{1,0:T(8,128)(2,1)} fusion(bf16[384,384]{1,0:T(8,128)(2,1)S(1)} %get-tuple-element.21, bf16[1,384,1536]{2,1,0:T(8,128)(2,1)} %all-gather.11.cloned.1.call-done), kind=kOutput, calls=%fused_computation.7 | convolution fusion | flops 453574656 | bytes 2654208 | tf_op jit(solution)/shard_map/rf,fd->rd/dot_general | solution.py:52
  67.4 12.6 %all-to-all-done.1 = bf16[8,48,1536]{2,1,0:T(8,128)(2,1)S(1)} async-done(((bf16[8,48,1536]{2,1,0:T(8,128)(2,1)}), bf16[8,48,1536]{2,1,0:T(8,128)(2,1)S(1)}, u32[]{:S(2)}, u32[]{:S(2)}) %all-to-all-start.1) | async-done | bytes 1179680 | tf_op jit(solution)/shard_map/all_to_all | solution.py:31
  80.0 1.8 %convolution_convert_fusion.2 = bf16[384,1536]{1,0:T(8,128)(2,1)} fusion(bf16[384,384]{1,0:T(8,128)(2,1)S(1)} %get-tuple-element.21, bf16[384,1536]{1,0:T(8,128)(2,1)S(1)} %bitcast.77), kind=kOutput, calls=%fused_computation.4 | convolution fusion | flops 453574656 | bytes 2654208 | tf_op jit(solution)/shard_map/rf,rd->fd/dot_general | solution.py:66
  81.9 2.5 %multiply_convert_fusion = (bf16[384,384]{1,0:T(8,128)(2,1)S(1)}, bf16[384,384]{1,0:T(8,128)(2,1)S(1)}) fusion(f32[384,384]{1,0:T(8,128)} %fusion.9, f32[384,384]{1,0:T(8,128)} %get-tuple-element.22, bf16[384,1536]{1,0:T(8,128)(2,1)S(1)} %bitcast.78, bf16[1,384,1536]{2,1,0:T(8,128)(2,1)} %all-gather.11.cloned.1.call-done), kind=kOutput, calls=%fused_computation.24 | convolution fusion | flops 454901760 | bytes 4128768 | tf_op jit(solution)/shard_map/rd,fd->rf/dot_general | solution.py:56
  84.4 0.7 copy-done.3
  85.2 1.9 %convolution_convert_fusion.4 = bf16[384,1536]{1,0:T(8,128)(2,1)} fusion(bf16[384,384]{1,0:T(8,128)(2,1)S(1)} %get-tuple-element.14, bf16[384,1536]{1,0:T(8,128)(2,1)S(1)} %bitcast.73), kind=kOutput, calls=%fused_computation.6 | convolution fusion | flops 453574656 | bytes 2654208 | tf_op jit(solution)/shard_map/rf,rd->fd/dot_general | solution.py:66
  87.1 3.7 %all-to-all-start.2 = ((bf16[8,48,1536]{2,1,0:T(8,128)(2,1)}), bf16[8,48,1536]{2,1,0:T(8,128)(2,1)S(1)}, u32[]{:S(2)}, u32[]{:S(2)}) async-start(bf16[8,48,1536]{2,1,0:T(8,128)(2,1)} %bitcast.76), calls=%async_computation.2 | async-start | bytes 2359296 | tf_op jit(solution)/shard_map/all_to_all | solution.py:31
  90.8 1.9 %convolution_convert_fusion.3 = bf16[384,1536]{1,0:T(8,128)(2,1)} fusion(bf16[384,384]{1,0:T(8,128)(2,1)S(1)} %get-tuple-element.13, bf16[384,1536]{1,0:T(8,128)(2,1)S(1)} %bitcast.74), kind=kOutput, calls=%fused_computation.5 | convolution fusion | flops 453574656 | bytes 2654208 | tf_op jit(solution)/shard_map/rf,rd->fd/dot_general | solution.py:66
  92.6 2.2 %fusion.7 = f32[384,1536]{1,0:T(8,128)S(1)} fusion(bf16[384,384]{1,0:T(8,128)(2,1)} %copy-done.3, bf16[1,384,1536]{2,1,0:T(8,128)(2,1)} %all-gather.7.cloned.1.call-done), kind=kOutput, calls=%fused_computation.15 | convolution fusion | flops 452984832 | bytes 3833856 | tf_op jit(solution)/shard_map/rf,fd->rd/dot_general | solution.py:60
  94.9 1.8 %fusion = bf16[384,1536]{1,0:T(8,128)(2,1)} fusion(f32[384,1536]{1,0:T(8,128)S(1)} %fusion.7, bf16[384,384]{1,0:T(8,128)(2,1)S(1)} %get-tuple-element.13, bf16[1,384,1536]{2,1,0:T(8,128)(2,1)S(1)} %copy-done.2), kind=kOutput, calls=%fused_computation.1 | convolution fusion | flops 454164480 | bytes 5013504 | tf_op jit(solution)/shard_map/rf,fd->rd/dot_general | solution.py:61
  96.7 22.8 %all-to-all-done.2 = bf16[8,48,1536]{2,1,0:T(8,128)(2,1)S(1)} async-done(((bf16[8,48,1536]{2,1,0:T(8,128)(2,1)}), bf16[8,48,1536]{2,1,0:T(8,128)(2,1)S(1)}, u32[]{:S(2)}, u32[]{:S(2)}) %all-to-all-start.2) | async-done | bytes 1179680 | tf_op jit(solution)/shard_map/all_to_all | solution.py:31
  119.5 3.8 %all-to-all-start.3 = ((bf16[8,48,1536]{2,1,0:T(8,128)(2,1)}), bf16[8,48,1536]{2,1,0:T(8,128)(2,1)S(1)}, u32[]{:S(2)}, u32[]{:S(2)}) async-start(bf16[8,48,1536]{2,1,0:T(8,128)(2,1)} %bitcast.15), calls=%async_computation.3 | async-start | bytes 2359296 | tf_op jit(solution)/shard_map/all_to_all | solution.py:31
  123.3 0.4 fusion.14
  123.6 1.2 fusion.11
  124.8 0.6 pad_maximum_fusion
  125.4 26.6 %all-to-all-done.3 = bf16[8,48,1536]{2,1,0:T(8,128)(2,1)S(1)} async-done(((bf16[8,48,1536]{2,1,0:T(8,128)(2,1)}), bf16[8,48,1536]{2,1,0:T(8,128)(2,1)S(1)}, u32[]{:S(2)}, u32[]{:S(2)}) %all-to-all-start.3) | async-done | bytes 1179680 | tf_op jit(solution)/shard_map/all_to_all | solution.py:31
  152.0 1.1 convolution_convert_fusion.6
  (29 shorter events, 0.6 us)
Async XLA Ops:
  7.2 3.1 %copy-start = (bf16[128,1536]{1,0:T(8,128)(2,1)S(1)}, bf16[128,1536]{1,0:T(8,128)(2,1)}, u32[]{:S(2)}) copy-start(bf16[128,1536]{1,0:T(8,128)(2,1)} %param.7) | copy-start | bytes 1179652
  11.8 35.8 %all-to-all-start = ((bf16[8,48,1536]{2,1,0:T(8,128)(2,1)}), bf16[8,48,1536]{2,1,0:T(8,128)(2,1)S(1)}, u32[]{:S(2)}, u32[]{:S(2)}) async-start(bf16[8,48,1536]{2,1,0:T(8,128)(2,1)} %bitcast.3), calls=%async_computation | async-start | bytes 2359296 | tf_op jit(solution)/shard_map/all_to_all | solution.py:31
  19.1 1.5 copy-start.5
  19.1 1.7 %copy-start.1 = (bf16[128,1536]{1,0:T(8,128)(2,1)S(1)}, bf16[128,1536]{1,0:T(8,128)(2,1)}, u32[]{:S(2)}) copy-start(bf16[128,1536]{1,0:T(8,128)(2,1)} %param.10) | copy-start | bytes 1179652
  19.1 33.0 %all-gather.7.cloned.1.call-start = ((), (), s32[]{:S(2)}) async-start(), calls=%async_computation.10 | async-start | bytes 1769472 | tf_op jit(solution)/shard_map/all_gather | solution.py:44
  19.8 35.2 %all-gather.9.cloned.1.call-start = ((), (), s32[]{:S(2)}) async-start(), calls=%async_computation.11 | async-start | bytes 1769472 | tf_op jit(solution)/shard_map/all_gather | solution.py:45
  47.6 32.4 %all-to-all-start.1 = ((bf16[8,48,1536]{2,1,0:T(8,128)(2,1)}), bf16[8,48,1536]{2,1,0:T(8,128)(2,1)S(1)}, u32[]{:S(2)}, u32[]{:S(2)}) async-start(bf16[8,48,1536]{2,1,0:T(8,128)(2,1)} %bitcast.9), calls=%async_computation.1 | async-start | bytes 2359296 | tf_op jit(solution)/shard_map/all_to_all | solution.py:31
  51.3 13.1 %all-gather.11.cloned.1.call-start = ((), (), s32[]{:S(2)}) async-start(), calls=%async_computation.12 | async-start | bytes 1769472 | tf_op jit(solution)/shard_map/all_gather | solution.py:46
  52.0 101.1 %reduce-scatter.8.cloned.1.call-start = ((), (), s32[]{:S(2)}) async-start(), calls=%async_computation.9 | async-start | bytes 1769472 | tf_op jit(solution)/shard_map/reduce_scatter | solution.py:67
  81.9 71.2 %reduce-scatter.4.cloned.1.call-start = ((), (), s32[]{:S(2)}) async-start(), calls=%async_computation.7 | async-start | bytes 1769472 | tf_op jit(solution)/shard_map/reduce_scatter | solution.py:67
  84.4 0.7 copy-start.3
  87.1 32.4 %all-to-all-start.2 = ((bf16[8,48,1536]{2,1,0:T(8,128)(2,1)}), bf16[8,48,1536]{2,1,0:T(8,128)(2,1)S(1)}, u32[]{:S(2)}, u32[]{:S(2)}) async-start(bf16[8,48,1536]{2,1,0:T(8,128)(2,1)} %bitcast.76), calls=%async_computation.2 | async-start | bytes 2359296 | tf_op jit(solution)/shard_map/all_to_all | solution.py:31
  90.7 62.4 %reduce-scatter.6.cloned.1.call-start = ((), (), s32[]{:S(2)}) async-start(), calls=%async_computation.8 | async-start | bytes 1769472 | tf_op jit(solution)/shard_map/reduce_scatter | solution.py:67
  92.6 2.2 %copy-start.2 = (bf16[1,384,1536]{2,1,0:T(8,128)(2,1)S(1)}, bf16[1,384,1536]{2,1,0:T(8,128)(2,1)}, u32[]{:S(2)}) copy-start(bf16[1,384,1536]{2,1,0:T(8,128)(2,1)} %all-gather.9.cloned.1.call-done) | copy-start | bytes 3538948
  119.5 3.8 %copy-start.4 = (pred[2,128,384]{2,1,0:T(32,128)(4,1)S(1)}, pred[2,128,384]{2,1,0:T(32,128)(4,1)}, u32[]{:S(2)}) copy-start(pred[2,128,384]{2,1,0:T(32,128)(4,1)} %get-tuple-element.17) | copy-start | bytes 294916
  119.5 32.5 %all-to-all-start.3 = ((bf16[8,48,1536]{2,1,0:T(8,128)(2,1)}), bf16[8,48,1536]{2,1,0:T(8,128)(2,1)S(1)}, u32[]{:S(2)}, u32[]{:S(2)}) async-start(bf16[8,48,1536]{2,1,0:T(8,128)(2,1)} %bitcast.15), calls=%async_computation.3 | async-start | bytes 2359296 | tf_op jit(solution)/shard_map/all_to_all | solution.py:31
Sparse Core Ops, SparseCore 0:
  21.5 10.6 all-gather.6
  33.7 10.3 all-gather.8
  53.7 10.6 all-gather.10
  82.0 7.7 reduce-scatter.7
  92.6 9.8 reduce-scatter.3
  105.1 9.8 reduce-scatter.5

commit v4 on v3

--- a/solution.py
+++ b/solution.py
@@ -1,7 +1,145 @@
+import functools
+
 import jax
 import jax.numpy as jnp
 from jax import lax
+from jax.experimental import pallas as pl
+from jax.experimental.pallas import tpu as pltpu
 from jax.sharding import PartitionSpec as P
+
+
+def dot(left, right, dims=((1,), (0,))):
+    return lax.dot_general(left, right, (dims, ((), ())), preferred_element_type=jnp.float32)
+
+
+def fused(
+    experts, replicas, capacity,
+    send_x, send_dy, gate_in, up_in, down_in, pick0, pick1, place, weights, cotangent,
+    mixed, token_grad, route_grad, gate_grad, up_grad, down_grad,
+    recv_x, recv_dy, out_send, grad_send, back_out, back_grad,
+    w_full, factor_gate, factor_up, hidden, gate_delta, up_delta, turned,
+    part_send, part_recv, part_own,
+    row_send, row_recv, core_send, core_recv,
+):
+    f32, bf16 = jnp.float32, jnp.bfloat16
+    me = lax.axis_index("expert") * replicas + lax.axis_index("dp")
+    core = lax.axis_index("sub")
+    half = gate_in.shape[0]
+    mesh_id = pl.DeviceIdType.MESH
+
+    def device(index):
+        return {"expert": lax.div(index, replicas), "dp": lax.rem(index, replicas)}
+
+    barrier = pltpu.get_barrier_semaphore()
+    for r in range(1, experts):
+        pl.semaphore_signal(
+            barrier, inc=1, device_id=device(lax.rem(me + r, experts)), device_id_type=mesh_id
+        )
+    pl.semaphore_signal(barrier, inc=1, device_id={"sub": 1 - core}, device_id_type=mesh_id)
+    pl.semaphore_wait(barrier, experts)
+
+    def block(index):
+        return pl.ds(pl.multiple_of(index * capacity, 16), capacity)
+
+    def unit_rows(index):
+        return pl.ds(pl.multiple_of(index * half, 16), half)
+
+    def exchange(which, source, landing):
+        copies = []
+        for r in range(1, experts):
+            to = lax.rem(me + r, experts)
+            copy = pltpu.make_async_remote_copy(
+                src_ref=source.at[block(to)],
+                dst_ref=landing.at[block(me)],
+                send_sem=row_send.at[which, r],
+                recv_sem=row_recv.at[which, r],
+                device_id=device(to),
+                device_id_type=mesh_id,
+            )
+            copy.start()
+            copies.append(copy)
+        landing[block(me), :] = source[block(me), :]
+        return copies
+
+    def to_core(slot, source, landing):
+        copy = pltpu.make_async_remote_copy(
+            src_ref=source,
+            dst_ref=landing,
+            send_sem=core_send.at[slot],
+            recv_sem=core_recv.at[slot],
+            device_id={"sub": 1 - core},
+            device_id_type=mesh_id,
+        )
+        copy.start()
+        return copy
+
+    def finish(copies):
+        for copy in copies:
+            copy.wait()
+
+    x_copies = exchange(0, send_x, recv_x)
+    w_copies = []
+    for k, ref in enumerate((gate_in, up_in, down_in)):
+        w_copies.append(to_core(k, ref, w_full.at[k, unit_rows(core)]))
+        w_full[k, unit_rows(core), :] = ref[...]
+    dy_copies = exchange(1, send_dy, recv_dy)
+    finish(w_copies)
+    finish(x_copies)
+
+    total = recv_x.shape[0]
+    step = total // 2
+
+    def forward(i, carry):
+        rows = pl.ds(pl.multiple_of(i * step, 16), step)
+        x = recv_x[rows, :]
+        gate = dot(x, w_full[0], ((1,), (1,)))
+        up = dot(x, w_full[1], ((1,), (1,)))
+        sigmoid = jax.nn.sigmoid(gate)
+        act = gate * sigmoid
+        rounded = (act * up).astype(bf16)
+        hidden[rows, :] = rounded
+        factor_gate[rows, :] = up * sigmoid * (1.0 + gate * (1.0 - sigmoid))
+        factor_up[rows, :] = act
+        out_send[rows, :] = dot(rounded, w_full[2]).astype(bf16)
+        return carry
+
+    lax.fori_loop(0, 2, forward, 0)
+    out_copies = exchange(2, out_send, back_out)
+    finish(dy_copies)
+
+    def backward(i, carry):
+        rows = pl.ds(pl.multiple_of(i * step, 16), step)
+        back = dot(recv_dy[rows, :], w_full[2], ((1,), (1,)))
+        by_gate = (back * factor_gate[rows, :]).astype(bf16)
+        by_up = (back * factor_up[rows, :]).astype(bf16)
+        gate_delta[rows, :] = by_gate
+        up_delta[rows, :] = by_up
+        grad_send[rows, :] = (dot(by_gate, w_full[0]) + dot(by_up, w_full[1])).astype(bf16)
+        return carry
+
+    lax.fori_loop(0, 2, backward, 0)
+    grad_copies = exchange(3, grad_send, back_grad)
+
+    part_copies = []
+    sides = ((hidden, recv_dy), (gate_delta, recv_x), (up_delta, recv_x))
+    for k, (left, right) in enumerate(sides):
+        turned[...] = left[...].astype(f32).T.astype(bf16)
+        part_send[k] = dot(turned[unit_rows(1 - core), :], right[...]).astype(bf16)
+        part_copies.append(to_core(3 + k, part_send.at[k], part_recv.at[k]))
+        part_own[k] = dot(turned[unit_rows(core), :], right[...]).astype(bf16)
+    finish(part_copies)
+    for k, ref in enumerate((down_grad, gate_grad, up_grad)):
+        ref[...] = (part_own[k].astype(f32) + part_recv[k].astype(f32)).astype(bf16)
+
+    finish(out_copies)
+    dy = cotangent[...].astype(f32)
+    first = dot(pick0[...], back_out[...])
+    second = dot(pick1[...], back_out[...])
+    mixed[...] = (weights[:, 0:1] * first + weights[:, 1:2] * second).astype(bf16)
+    route_grad[:, 0:1] = jnp.sum(dy * first, axis=1, keepdims=True)
+    route_grad[:, 1:2] = jnp.sum(dy * second, axis=1, keepdims=True)
+    finish(grad_copies)
+    token_grad[...] = dot(place[...], back_grad[...]).astype(bf16)
 
 
 def shards(tokens, expert_ids, route_weights, out_grad, gate_weight, up_weight, down_weight):
@@ -38,8 +176,40 @@
         return moved.reshape(rows_total, features)
 
     send_x = jnp.einsum("ts,td->sd", place, tokens, preferred_element_type=f32).astype(bf16)
+    send_dy = jnp.einsum("ts,td->sd", weigh, out_grad, preferred_element_type=f32).astype(bf16)
+    if capacity % 16 == 0 and experts <= 8 and lax.axis_size("sub") == 2 and top_count == 2:
+        units = 2 * gate_weight.shape[1]
+        half = gate_weight.shape[1]
+        vmem = pl.BlockSpec(memory_space=pltpu.VMEM)
+        slab = pltpu.VMEM((rows_total, features), bf16)
+        wide = pltpu.VMEM((rows_total, units), f32)
+        slim = pltpu.VMEM((rows_total, units), bf16)
+        part = pltpu.VMEM((3, half, features), bf16)
+        like = jax.ShapeDtypeStruct
+        results = pl.pallas_call(
+            functools.partial(fused, experts, lax.axis_size("dp"), capacity),
+            out_shape=(
+                like((tok_rows, features), bf16),
+                like((tok_rows, features), bf16),
+                like((tok_rows, top_count), f32),
+            )
+            + (like((half, features), bf16),) * 3,
+            in_specs=[vmem] * 10,
+            out_specs=(vmem,) * 6,
+            scratch_shapes=[slab] * 6
+            + [pltpu.VMEM((3, units, features), bf16), wide, wide, slim, slim, slim]
+            + [pltpu.VMEM((units, rows_total), bf16), part, part, part]
+            + [pltpu.SemaphoreType.DMA((4, experts))] * 2
+            + [pltpu.SemaphoreType.DMA((6,))] * 2,
+            compiler_params=pltpu.CompilerParams(
+                collective_id=0, has_side_effects=True, vmem_limit_bytes=48 * 1024 * 1024
+            ),
+        )(
+            send_x, send_dy, gate_weight[0], up_weight[0], down_weight[0],
+            pick[0], pick[1], place, route_weights.astype(f32), out_grad,
+        )
+        return results[:3] + tuple(r[None] for r in results[3:])
     recv_x = exchange(send_x)
-    send_dy = jnp.einsum("ts,td->sd", weigh, out_grad, preferred_element_type=f32).astype(bf16)
     recv_dy = exchange(send_dy)
     gate_full = lax.all_gather(gate_weight[0], "sub", axis=0, tiled=True)
     up_full = lax.all_gather(up_weight[0], "sub", axis=0, tiled=True)

time: 161 us -> 121 us (0.75)
  the two profiles are of different devices: /device:TPU:0 before, /device:TPU:11 now
where the time goes in v4:
time: 121 us
  Pallas kernels  109 us (90%)
  local copies, waits for them, and re-layouts  5.46 us (5%)
  matrix products  3.2 us (3%)
  other arithmetic  2.47 us (2%)
    pallas_call x1, Pallas kernels, shards(): pl.pallas_call(functools.partial(fused, experts, lax.axis_size('dp'), cap...  109 us
    unnamed x17, local copies, waits for them, and re-layouts  5.38 us

profile of v4, /device:TPU:11, one launch (start us, length us, event | category | flops | bytes accessed | tf_op | source)
XLA Modules:
  0.0 120.7 jit_solution(8691956774771003060)
XLA Ops:
  0.6 0.0 copy-start
  0.6 0.0 copy-start.1
  0.7 0.8 fusion.4
  1.4 0.1 fusion.3
  1.5 0.7 select_reduce_fusion.1
  2.3 0.7 add_bitcast_fusion
  2.9 0.8 copy.18
  3.7 0.1 copy.19
  3.8 0.2 select_reduce_fusion
  4.0 0.1 fusion
  4.2 0.0 copy-done.1
  4.2 0.0 copy-start.4
  4.2 1.5 %convolution_convert_fusion.send_dy = bf16[384,1536]{1,0:T(8,128)(2,1)} fusion(bf16[128,1536]{1,0:T(8,128)(2,1)S(1)} %copy-done.1, bf16[128,384]{1,0:T(8,128)(2,1)S(1)} %select_reduce_fusion), kind=kOutput, calls=%fused_computation | convolution fusion | flops 151584768 | bytes 1671168 | tf_op jit(solution)/shard_map/ts,td->sd/dot_general | solution.py:179
  5.7 0.0 copy-done
  5.7 0.0 copy-start.2
  5.7 0.0 copy-start.3
  5.7 1.5 %convolution_convert_fusion.1.send_x = bf16[384,1536]{1,0:T(8,128)(2,1)} fusion(pred[128,384]{1,0:T(8,128)(4,1)S(1)} %get-tuple-element.35, bf16[128,1536]{1,0:T(8,128)(2,1)S(1)} %copy-done), kind=kOutput, calls=%fused_computation.1 | convolution fusion | flops 151584768 | bytes 1622016 | tf_op jit(solution)/shard_map/ts,td->sd/dot_general | solution.py:178
  7.3 0.0 copy-done.4
  7.3 0.0 copy-done.2
  7.3 0.0 copy-done.3
  7.3 108.8 %shard_map.118 = (bf16[128,1536]{1,0:T(8,128)(2,1)S(1)}, bf16[128,1536]{1,0:T(8,128)(2,1)S(1)}, f32[128,2]{1,0:T(8,128)S(1)}, bf16[192,1536]{1,0:T(8,128)(2,1)S(...) custom-call(bf16[384,1536]{1,0:T(8,128)(2,1)} %convolution_convert_fusion.1.send_x, ...), custom_call_target="tpu_custom_call" | custom-call | tf_op jit(solution)/shard_map/pallas_call | solution.py:189
  116.1 0.6 copy.20
  116.8 0.7 copy.26
  117.5 0.7 copy.27
  118.2 0.8 copy.28
  119.1 0.8 copy.29
  119.9 0.8 copy.30
  (3 shorter events, 0.0 us)
Async XLA Ops:
  0.6 5.1 %copy-start = (bf16[128,1536]{1,0:T(8,128)(2,1)S(1)}, bf16[128,1536]{1,0:T(8,128)(2,1)}, u32[]{:S(2)}) copy-start(bf16[128,1536]{1,0:T(8,128)(2,1)} %param.7) | copy-start | bytes 1179652
  0.6 3.5 %copy-start.1 = (bf16[128,1536]{1,0:T(8,128)(2,1)S(1)}, bf16[128,1536]{1,0:T(8,128)(2,1)}, u32[]{:S(2)}) copy-start(bf16[128,1536]{1,0:T(8,128)(2,1)} %cotangent.1) | copy-start | bytes 1179652
  4.2 3.1 %copy-start.4 = (bf16[1,192,1536]{2,1,0:T(8,128)(2,1)S(1)}, bf16[1,192,1536]{2,1,0:T(8,128)(2,1)}, u32[]{:S(2)}) copy-start(bf16[1,192,1536]{2,1,0:T(8,128)(2,1)} %param.13) | copy-start | bytes 1769476
  5.7 1.5 %copy-start.2 = (bf16[1,192,1536]{2,1,0:T(8,128)(2,1)S(1)}, bf16[1,192,1536]{2,1,0:T(8,128)(2,1)}, u32[]{:S(2)}) copy-start(bf16[1,192,1536]{2,1,0:T(8,128)(2,1)} %param.11) | copy-start | bytes 1769476
  5.7 1.5 %copy-start.3 = (bf16[1,192,1536]{2,1,0:T(8,128)(2,1)S(1)}, bf16[1,192,1536]{2,1,0:T(8,128)(2,1)}, u32[]{:S(2)}) copy-start(bf16[1,192,1536]{2,1,0:T(8,128)(2,1)} %param.12) | copy-start | bytes 1769476

commit v5 on v4

--- a/solution.py
+++ b/solution.py
@@ -14,9 +14,9 @@
 
 def fused(
     experts, replicas, capacity,
-    send_x, send_dy, gate_in, up_in, down_in, pick0, pick1, place, weights, cotangent,
+    tokens, cotangent, gate_in, up_in, down_in, target, target_t, weights, weights_t,
     mixed, token_grad, route_grad, gate_grad, up_grad, down_grad,
-    recv_x, recv_dy, out_send, grad_send, back_out, back_grad,
+    place_t, weigh_t, send_x, send_dy, recv_x, recv_dy, out_send, grad_send, back_out, back_grad,
     w_full, factor_gate, factor_up, hidden, gate_delta, up_delta, turned,
     part_send, part_recv, part_own,
     row_send, row_recv, core_send, core_recv,
@@ -31,11 +31,24 @@
         return {"expert": lax.div(index, replicas), "dp": lax.rem(index, replicas)}
 
     barrier = pltpu.get_barrier_semaphore()
+    def peer(r):
+        index, bit = 0, 1
+        while bit < experts:
+            own = lax.rem(lax.div(me, bit), 2)
+            index = index + bit * (1 - own if r & bit else own)
+            bit *= 2
+        return index
+
     for r in range(1, experts):
-        pl.semaphore_signal(
-            barrier, inc=1, device_id=device(lax.rem(me + r, experts)), device_id_type=mesh_id
-        )
+        pl.semaphore_signal(barrier, inc=1, device_id=device(peer(r)), device_id_type=mesh_id)
     pl.semaphore_signal(barrier, inc=1, device_id={"sub": 1 - core}, device_id_type=mesh_id)
+
+    slot = lax.broadcasted_iota(jnp.int32, place_t.shape, 0)
+    at_first, at_second = slot == target_t[0:1, :], slot == target_t[1:2, :]
+    place_t[...] = jnp.where(at_first | at_second, 1.0, 0.0).astype(bf16)
+    weigh_t[...] = jnp.where(
+        at_first, weights_t[0:1, :], jnp.where(at_second, weights_t[1:2, :], 0.0)
+    ).astype(bf16)
     pl.semaphore_wait(barrier, experts)
 
     def block(index):
@@ -44,10 +57,12 @@
     def unit_rows(index):
         return pl.ds(pl.multiple_of(index * half, 16), half)
 
-    def exchange(which, source, landing):
+    def exchange(which, source, landing, fill=None):
         copies = []
-        for r in range(1, experts):
-            to = lax.rem(me + r, experts)
+        for r in range(experts - 1, 0, -1):
+            to = peer(r)
+            if fill is not None:
+                fill(to)
             copy = pltpu.make_async_remote_copy(
                 src_ref=source.at[block(to)],
                 dst_ref=landing.at[block(me)],
@@ -58,6 +73,8 @@
             )
             copy.start()
             copies.append(copy)
+        if fill is not None:
+            fill(me)
         landing[block(me), :] = source[block(me), :]
         return copies
 
@@ -77,12 +94,18 @@
         for copy in copies:
             copy.wait()
 
-    x_copies = exchange(0, send_x, recv_x)
+    def fill_x(e):
+        send_x[block(e), :] = dot(place_t[block(e), :], tokens[...]).astype(bf16)
+
+    def fill_dy(e):
+        send_dy[block(e), :] = dot(weigh_t[block(e), :], cotangent[...]).astype(bf16)
+
+    x_copies = exchange(0, send_x, recv_x, fill_x)
     w_copies = []
     for k, ref in enumerate((gate_in, up_in, down_in)):
         w_copies.append(to_core(k, ref, w_full.at[k, unit_rows(core)]))
         w_full[k, unit_rows(core), :] = ref[...]
-    dy_copies = exchange(1, send_dy, recv_dy)
+    dy_copies = exchange(1, send_dy, recv_dy, fill_dy)
     finish(w_copies)
     finish(x_copies)
 
@@ -133,13 +156,16 @@
 
     finish(out_copies)
     dy = cotangent[...].astype(f32)
-    first = dot(pick0[...], back_out[...])
-    second = dot(pick1[...], back_out[...])
+    lane = lax.broadcasted_iota(jnp.int32, (target.shape[0], total), 1)
+    pick0 = jnp.where(lane == target[:, 0:1], 1.0, 0.0)
+    pick1 = jnp.where(lane == target[:, 1:2], 1.0, 0.0)
+    first = dot(pick0.astype(bf16), back_out[...])
+    second = dot(pick1.astype(bf16), back_out[...])
     mixed[...] = (weights[:, 0:1] * first + weights[:, 1:2] * second).astype(bf16)
     route_grad[:, 0:1] = jnp.sum(dy * first, axis=1, keepdims=True)
     route_grad[:, 1:2] = jnp.sum(dy * second, axis=1, keepdims=True)
     finish(grad_copies)
-    token_grad[...] = dot(place[...], back_grad[...]).astype(bf16)
+    token_grad[...] = dot((pick0 + pick1).astype(bf16), back_grad[...]).astype(bf16)
 
 
 def shards(tokens, expert_ids, route_weights, out_grad, gate_weight, up_weight, down_weight):
@@ -157,27 +183,7 @@
     before = jnp.dot(earlier, named, preferred_element_type=f32)
     slot_index = jnp.sum(jnp.where(hit, before[:, None, :], 0.0), axis=2).astype(jnp.int32)
     target = expert_ids * capacity + slot_index
-    slots = jnp.arange(rows_total, dtype=jnp.int32)
-    picks = target.T[:, :, None] == slots[None, None, :]
-    pick = picks.astype(bf16)
-    place = jnp.any(picks, axis=0).astype(bf16)
-    weigh = jnp.sum(
-        jnp.where(picks, route_weights.T.astype(f32)[:, :, None], 0.0), axis=0
-    ).astype(bf16)
-
-    def exchange(rows):
-        moved = lax.all_to_all(
-            rows.reshape(experts, capacity, features),
-            ("expert", "dp"),
-            split_axis=0,
-            concat_axis=0,
-            tiled=True,
-        )
-        return moved.reshape(rows_total, features)
-
-    send_x = jnp.einsum("ts,td->sd", place, tokens, preferred_element_type=f32).astype(bf16)
-    send_dy = jnp.einsum("ts,td->sd", weigh, out_grad, preferred_element_type=f32).astype(bf16)
-    if capacity % 16 == 0 and experts <= 8 and lax.axis_size("sub") == 2 and top_count == 2:
+    if capacity % 16 == 0 and experts in (2, 4, 8) and lax.axis_size("sub") == 2 and top_count == 2:
         units = 2 * gate_weight.shape[1]
         half = gate_weight.shape[1]
         vmem = pl.BlockSpec(memory_space=pltpu.VMEM)
@@ -194,9 +200,9 @@
                 like((tok_rows, top_count), f32),
             )
             + (like((half, features), bf16),) * 3,
-            in_specs=[vmem] * 10,
+            in_specs=[vmem] * 9,
             out_specs=(vmem,) * 6,
-            scratch_shapes=[slab] * 6
+            scratch_shapes=[pltpu.VMEM((rows_total, tok_rows), bf16)] * 2 + [slab] * 8
             + [pltpu.VMEM((3, units, features), bf16), wide, wide, slim, slim, slim]
             + [pltpu.VMEM((units, rows_total), bf16), part, part, part]
             + [pltpu.SemaphoreType.DMA((4, experts))] * 2
@@ -205,10 +211,31 @@
                 collective_id=0, has_side_effects=True, vmem_limit_bytes=48 * 1024 * 1024
             ),
         )(
-            send_x, send_dy, gate_weight[0], up_weight[0], down_weight[0],
-            pick[0], pick[1], place, route_weights.astype(f32), out_grad,
+            tokens, out_grad, gate_weight[0], up_weight[0], down_weight[0],
+            target, target.T, route_weights.astype(f32), route_weights.T.astype(f32),
         )
         return results[:3] + tuple(r[None] for r in results[3:])
+
+    slots = jnp.arange(rows_total, dtype=jnp.int32)
+    picks = target.T[:, :, None] == slots[None, None, :]
+    pick = picks.astype(bf16)
+    place = jnp.any(picks, axis=0).astype(bf16)
+    weigh = jnp.sum(
+        jnp.where(picks, route_weights.T.astype(f32)[:, :, None], 0.0), axis=0
+    ).astype(bf16)
+
+    def exchange(rows):
+        moved = lax.all_to_all(
+            rows.reshape(experts, capacity, features),
+            ("expert", "dp"),
+            split_axis=0,
+            concat_axis=0,
+            tiled=True,
+        )
+        return moved.reshape(rows_total, features)
+
+    send_x = jnp.einsum("ts,td->sd", place, tokens, preferred_element_type=f32).astype(bf16)
+    send_dy = jnp.einsum("ts,td->sd", weigh, out_grad, preferred_element_type=f32).astype(bf16)
     recv_x = exchange(send_x)
     recv_dy = exchange(send_dy)
     gate_full = lax.all_gather(gate_weight[0], "sub", axis=0, tiled=True)

time: 121 us -> 122 us (level)
  the two profiles are of different devices: /device:TPU:11 before, /device:TPU:0 now
where the time goes in v5:
time: 122 us
  Pallas kernels  110 us (90%)
  local copies, waits for them, and re-layouts  11.3 us (9%)
    pallas_call x1, Pallas kernels, shards(): pl.pallas_call(functools.partial(fused, experts, lax.axis_size('dp'), cap...  110 us
    unnamed x20, local copies, waits for them, and re-layouts  11.1 us

profile of v5, /device:TPU:0, one launch (start us, length us, event | category | flops | bytes accessed | tf_op | source)
XLA Modules:
  0.0 121.9 jit_solution(8192660309711045498)
XLA Ops:
  0.6 0.0 copy-start.6
  0.6 0.6 copy-done.6
  1.3 0.0 copy-start.5
  1.3 0.7 copy-done.5
  2.0 0.1 fusion
  2.2 0.1 copy.18.target
  2.3 0.1 copy.19.weights
  2.4 0.0 copy-start
  2.4 1.1 copy-done
  3.5 0.0 copy-start.1
  3.5 1.1 copy-done.1
  4.5 0.0 copy-start.2
  4.5 1.1 copy-done.2
  5.6 0.0 copy-start.3
  5.6 1.0 copy-done.3
  6.6 0.0 copy-start.4
  6.6 1.0 copy-done.4
  7.6 109.7 %shard_map.118 = (bf16[128,1536]{1,0:T(8,128)(2,1)S(1)}, bf16[128,1536]{1,0:T(8,128)(2,1)S(1)}, f32[128,2]{1,0:T(8,128)S(1)}, bf16[192,1536]{1,0:T(8,128)(2,1)S(...) custom-call(bf16[128,1536]{1,0:T(8,128)(2,1)S(1)} %copy-done.3, bf16[128,1536]{1,0:T(8,128)(2,1)S(1)} %copy-done.4, ...), custom_call_target="tpu_custom_call" | custom-call | tf_op jit(solution)/shard_map/pallas_call | solution.py:195
  117.3 0.6 copy.20
  118.0 0.7 copy.26
  118.7 0.7 copy.27
  119.4 0.8 copy.28
  120.3 0.8 copy.29
  121.1 0.8 copy.30
  (4 shorter events, 0.0 us)
Async XLA Ops:
  0.6 0.7 copy-start.6
  1.3 0.7 copy-start.5
  2.4 1.1 copy-start
  3.5 1.1 copy-start.1
  4.5 1.1 copy-start.2
  5.6 1.0 copy-start.3
  6.6 1.0 copy-start.4

commit v6 on v5

--- a/solution.py
+++ b/solution.py
@@ -14,12 +14,12 @@
 
 def fused(
     experts, replicas, capacity,
-    tokens, cotangent, gate_in, up_in, down_in, target, target_t, weights, weights_t,
+    tokens_in, cotangent_in, gate_in, up_in, down_in, target, target_t, weights, weights_t,
     mixed, token_grad, route_grad, gate_grad, up_grad, down_grad,
     place_t, weigh_t, send_x, send_dy, recv_x, recv_dy, out_send, grad_send, back_out, back_grad,
     w_full, factor_gate, factor_up, hidden, gate_delta, up_delta, turned,
     part_send, part_recv, part_own,
-    row_send, row_recv, core_send, core_recv,
+    row_send, row_recv, core_send, core_recv, tokens, cotangent, loaded,
 ):
     f32, bf16 = jnp.float32, jnp.bfloat16
     me = lax.axis_index("expert") * replicas + lax.axis_index("dp")
@@ -32,12 +32,16 @@
 
     barrier = pltpu.get_barrier_semaphore()
     def peer(r):
-        index, bit = 0, 1
-        while bit < experts:
-            own = lax.rem(lax.div(me, bit), 2)
-            index = index + bit * (1 - own if r & bit else own)
-            bit *= 2
-        return index
+        return lax.rem(me + r, experts)
+
+    loads = []
+    sources = (tokens_in, cotangent_in, gate_in, up_in, down_in)
+    own_rows = pl.ds(pl.multiple_of(core * half, 16), half)
+    landings = (tokens, cotangent) + tuple(w_full.at[k, own_rows] for k in range(3))
+    for k in range(5):
+        load = pltpu.make_async_copy(sources[k], landings[k], loaded.at[k])
+        load.start()
+        loads.append(load)
 
     for r in range(1, experts):
         pl.semaphore_signal(barrier, inc=1, device_id=device(peer(r)), device_id_type=mesh_id)
@@ -59,7 +63,7 @@
 
     def exchange(which, source, landing, fill=None):
         copies = []
-        for r in range(experts - 1, 0, -1):
+        for r in range(1, experts):
             to = peer(r)
             if fill is not None:
                 fill(to)
@@ -100,13 +104,15 @@
     def fill_dy(e):
         send_dy[block(e), :] = dot(weigh_t[block(e), :], cotangent[...]).astype(bf16)
 
+    loads[0].wait()
     x_copies = exchange(0, send_x, recv_x, fill_x)
     w_copies = []
     for k, ref in enumerate((gate_in, up_in, down_in)):
         w_copies.append(to_core(k, ref, w_full.at[k, unit_rows(core)]))
-        w_full[k, unit_rows(core), :] = ref[...]
+    loads[1].wait()
     dy_copies = exchange(1, send_dy, recv_dy, fill_dy)
     finish(w_copies)
+    finish(loads[2:])
     finish(x_copies)
 
     total = recv_x.shape[0]
@@ -200,15 +206,17 @@
                 like((tok_rows, top_count), f32),
             )
             + (like((half, features), bf16),) * 3,
-            in_specs=[vmem] * 9,
+            in_specs=[pl.BlockSpec(memory_space=pltpu.HBM)] * 5 + [vmem] * 4,
             out_specs=(vmem,) * 6,
             scratch_shapes=[pltpu.VMEM((rows_total, tok_rows), bf16)] * 2 + [slab] * 8
             + [pltpu.VMEM((3, units, features), bf16), wide, wide, slim, slim, slim]
             + [pltpu.VMEM((units, rows_total), bf16), part, part, part]
             + [pltpu.SemaphoreType.DMA((4, experts))] * 2
-            + [pltpu.SemaphoreType.DMA((6,))] * 2,
+            + [pltpu.SemaphoreType.DMA((6,))] * 2
+            + [pltpu.VMEM((tok_rows, features), bf16)] * 2
+            + [pltpu.SemaphoreType.DMA((5,))],
             compiler_params=pltpu.CompilerParams(
-                collective_id=0, has_side_effects=True, vmem_limit_bytes=48 * 1024 * 1024
+                collective_id=0, has_side_effects=True, vmem_limit_bytes=60 * 1024 * 1024
             ),
         )(
             tokens, out_grad, gate_weight[0], up_weight[0], down_weight[0],

time: 122 us -> 122 us (level)
  the two profiles are of different devices: /device:TPU:0 before, /device:TPU:11 now
where the time goes in v6:
time: 122 us; the launch traced here: 121 us
  Pallas kernels  110 us (90%)
  local copies, waits for them, and re-layouts  10.1 us (8%)
    pallas_call x1, Pallas kernels, shards(): pl.pallas_call(functools.partial(fused, experts, lax.axis_size('dp'), cap...  110 us
    unnamed x20, local copies, waits for them, and re-layouts  8.64 us

profile of v6, /device:TPU:11, one launch (start us, length us, event | category | flops | bytes accessed | tf_op | source)
XLA Modules:
  0.0 121.2 jit_solution(12827068511355426729)
XLA Ops:
  0.6 0.0 copy-start.6
  0.6 0.6 copy-done.6
  1.3 0.0 copy-start.5
  1.3 0.6 convert_bitcast_fusion.weights_t
  1.9 0.1 copy-done.5
  2.0 0.1 fusion
  2.2 0.0 copy-start.4
  2.2 0.7 copy.18.target
  2.9 0.0 copy-done.4
  2.9 0.7 copy.19.weights
  3.7 109.7 %shard_map.118 = (bf16[128,1536]{1,0:T(8,128)(2,1)}, bf16[128,1536]{1,0:T(8,128)(2,1)}, f32[128,2]{1,0:T(8,128)}, bf16[192,1536]{1,0:T(8,128)(2,1)}, bf16[192,15...) custom-call(bf16[128,1536]{1,0:T(8,128)(2,1)} %tokens_in.1, bf16[128,1536]{1,0:T(8,128)(2,1)} %cotangent_in.1, ...), custom_call_target="tpu_custom_call" | custom-call | tf_op jit(solution)/shard_map/pallas_call | solution.py:201
  113.3 1.5 %copy.20 = f32[128,2]{0,1:T(2,128)} copy(f32[128,2]{1,0:T(8,128)} %get-tuple-element.26) | data formatting | bytes 2048
  114.8 0.0 copy-start.3
  114.8 1.8 %copy.26 = bf16[128,1536]{1,0:T(8,128)(2,1)} copy(bf16[128,1536]{1,0:T(8,128)(2,1)} %get-tuple-element.36) | data formatting | bytes 786432
  116.6 0.0 copy-done.3
  116.6 0.0 copy-start.2
  116.6 0.7 copy.27
  117.4 0.5 copy-done.2
  117.8 0.0 copy-start.1
  117.8 0.8 copy.28
  118.6 0.5 copy-done.1
  119.1 0.0 copy-start
  119.1 0.8 copy.29
  119.9 0.5 copy-done
  120.4 0.8 copy.30
  (3 shorter events, 0.0 us)
Async XLA Ops:
  0.6 0.7 copy-start.6
  1.3 0.7 copy-start.5
  2.2 0.8 copy-start.4
  114.8 1.8 %copy-start.3 = (bf16[128,1536]{1,0:T(8,128)(2,1)S(1)}, bf16[128,1536]{1,0:T(8,128)(2,1)}, u32[]{:S(2)}) copy-start(bf16[128,1536]{1,0:T(8,128)(2,1)} %get-tuple-element.37) | copy-start | bytes 1179652
  116.6 1.2 copy-start.2
  117.8 1.3 %copy-start.1 = (bf16[192,1536]{1,0:T(8,128)(2,1)S(1)}, bf16[192,1536]{1,0:T(8,128)(2,1)}, u32[]{:S(2)}) copy-start(bf16[192,1536]{1,0:T(8,128)(2,1)} %get-tuple-element.16) | copy-start | bytes 1769476
  119.1 1.3 %copy-start = (bf16[192,1536]{1,0:T(8,128)(2,1)S(1)}, bf16[192,1536]{1,0:T(8,128)(2,1)}, u32[]{:S(2)}) copy-start(bf16[192,1536]{1,0:T(8,128)(2,1)} %get-tuple-element.17) | copy-start | bytes 1769476
